TPU v7x, 32 devices: a whole 2x2x4 slice. The times are simulated.
32 devices in a mesh: rows: 16 (over z, y, core), blk: 2 (over x).
Axes of the slice: x: 2, y: 2, z: 4, core: 2. Of those that a mesh axis runs over, the one named last changes fastest.
Arguments:
- hidden: bfloat16 [16, 768, 1280], P('rows', 'blk'), may hold values from -6 to 6
- starts: int32 [16, 4], P('rows'), may hold values from 0 to 767, as said below
- first_gain: float32 [1280], replicated, may hold values from 0.5 to 2
- first_shift: float32 [1280], replicated, may hold values from -3 to 3
- qkv_weight: bfloat16 [1280, 3840], P('rows'), may hold values from -0.15625 to 0.15625
- out_weight: bfloat16 [1280, 1280], P('rows'), may hold values from -0.625 to 0.625
- second_gain: float32 [1280], replicated, may hold values from 0.5 to 2
- second_shift: float32 [1280], replicated, may hold values from -3 to 3
- up_weight: bfloat16 [1280, 5120], P('rows'), may hold values from -0.15625 to 0.15625
- hidden_bias: float32 [5120], replicated, may hold values from -3 to 3
- down_weight: bfloat16 [5120, 1280], P('rows'), may hold values from -0.078125 to 0.078125
- cotangent: bfloat16 [16, 768, 1280], P('rows', 'blk'), may hold values from -6 to 6
Outputs:
- output: float32 [16, 768, 1280], P('rows', 'blk')
- grad_hidden: float32 [16, 768, 1280], P('rows', 'blk')
- grad_qkv: float32 [1280, 3840], P('rows')
- grad_out: float32 [1280, 1280], P('rows')
- grad_up: float32 [1280, 5120], P('rows')
- grad_down: float32 [5120, 1280], P('rows')
- grad_first_gain: float32 [1280], replicated
- grad_first_shift: float32 [1280], replicated
- grad_second_gain: float32 [1280], replicated
- grad_second_shift: float32 [1280], replicated
- grad_hidden_bias: float32 [5120], replicated
Inputs may be any that keep to these rules, and one draw needn't show every extreme that they name: Each row of starts lists the first positions (CLS tokens) of its 4 cells in increasing order, beginning with 0; every cell holds one position or more, and a cell runs up to the next start (the last up to 768). In every row one cell begins among the first 384 positions and ends among the last 384.
All inputs are finite; a program needn't handle non-finite values.
Results may differ from a plain program's by a relative error of at most 0.02.
Values may be sent and summed in bfloat16 or wider, within the bound.
A program may use at most 256 MiB of HBM per device.

v0:
```python
import math

import jax
import jax.numpy as jnp
from jax import lax
from jax.experimental import pallas as pl
from jax.experimental.pallas import tpu as pltpu
from jax.sharding import PartitionSpec as P

HEADS = 20
HEAD_DIM = 64


masked_score = -1e30
block_limit = 512


def layer_norm(values, gain, shift):
    mean_value = jnp.mean(values, axis=-1, keepdims=True)
    centred = values - mean_value
    variance = jnp.mean(centred * centred, axis=-1, keepdims=True)
    return centred * lax.rsqrt(variance + 1e-05) * gain + shift


def segment_of(starts_row, positions):
    reached = starts_row[None, :] <= positions[:, None]
    return jnp.sum(reached.astype(jnp.int32), axis=1) - 1


def scores_with_mask(queries, key_block, query_seg, key_seg):
    products = jnp.einsum("qhe,khe->hqk", queries, key_block, preferred_element_type=jnp.float32)
    products = products * queries.shape[2] ** (-0.5)
    allowed = (query_seg[:, None] == key_seg[None, :])[None, :, :]
    return (jnp.where(allowed, products, masked_score), allowed)


def attend_rows(running, key_rows, value_rows, queries, query_seg, starts_row):
    piece_rows = key_rows.shape[0]
    step_rows = math.gcd(piece_rows, block_limit)
    head_count = queries.shape[1]
    head_width = queries.shape[2]

    def one_block(block_index, state):
        row_top, denominator, weighted = state
        block_start = block_index * step_rows
        key_block = lax.dynamic_slice_in_dim(key_rows, block_start, step_rows, 0).reshape(
            step_rows, head_count, head_width
        )
        value_block = lax.dynamic_slice_in_dim(value_rows, block_start, step_rows, 0).reshape(
            step_rows, head_count, head_width
        )
        key_seg = segment_of(starts_row, block_start + jnp.arange(step_rows, dtype=jnp.int32))
        scores, allowed = scores_with_mask(queries, key_block, query_seg, key_seg)
        new_top = jnp.maximum(row_top, jnp.max(scores, axis=-1))
        factor = jnp.exp(row_top - new_top)
        weights = jnp.where(allowed, jnp.exp(scores - new_top[:, :, None]), 0.0)
        denominator = denominator * factor + jnp.sum(weights, axis=-1)
        weighted = weighted * factor[:, :, None] + jnp.einsum(
            "hqk,khe->hqe",
            weights.astype(jnp.bfloat16),
            value_block,
            preferred_element_type=jnp.float32,
        )
        return (new_top, denominator, weighted)

    return lax.fori_loop(0, piece_rows // step_rows, one_block, running)


def on_device(
    hidden,
    starts,
    first_gain,
    first_shift,
    qkv_weight,
    out_weight,
    second_gain,
    second_shift,
    up_weight,
    hidden_bias,
    down_weight,
    cotangent,
):
    rows_here = hidden.shape[1]
    model_width = hidden.shape[2]
    head_count = HEADS
    head_width = HEAD_DIM
    score_scale = head_width ** (-0.5)
    inputs = hidden[0].astype(jnp.float32)
    starts_row = starts[0]
    offset = lax.axis_index("blk") * rows_here
    query_seg = segment_of(starts_row, offset + jnp.arange(rows_here, dtype=jnp.int32))
    qkv_full, out_full, up_full, down_full = (
        lax.all_gather(qkv_weight, "rows", axis=0, tiled=True),
        lax.all_gather(out_weight, "rows", axis=0, tiled=True),
        lax.all_gather(up_weight, "rows", axis=0, tiled=True),
        lax.all_gather(down_weight, "rows", axis=0, tiled=True),
    )
    normed_low = layer_norm(inputs, first_gain, first_shift).astype(jnp.bfloat16)
    packed = jnp.dot(normed_low, qkv_full, preferred_element_type=jnp.float32).astype(jnp.bfloat16)
    queries = packed[:, :model_width].reshape(rows_here, head_count, head_width)
    key_rows = packed[:, model_width : 2 * model_width]
    value_rows = packed[:, 2 * model_width :]
    initial = (
        jnp.full((head_count, rows_here), masked_score, jnp.float32),
        jnp.zeros((head_count, rows_here), jnp.float32),
        jnp.zeros((head_count, rows_here, head_width), jnp.float32),
    )
    row_top, denominator, weighted = attend_rows(
        initial,
        lax.all_gather(key_rows, "blk", axis=0, tiled=True),
        lax.all_gather(value_rows, "blk", axis=0, tiled=True),
        queries,
        query_seg,
        starts_row,
    )
    log_total = row_top + jnp.log(denominator)
    attended = jnp.transpose(weighted / denominator[:, :, None], (1, 0, 2))
    attended_low = attended.reshape(rows_here, model_width).astype(jnp.bfloat16)
    residual = inputs + jnp.dot(attended_low, out_full, preferred_element_type=jnp.float32)
    second_low = layer_norm(residual, second_gain, second_shift).astype(jnp.bfloat16)
    up_values = jnp.dot(second_low, up_full, preferred_element_type=jnp.float32) + hidden_bias
    activated_low = jax.nn.gelu(up_values, approximate=False).astype(jnp.bfloat16)
    output = residual + jnp.dot(activated_low, down_full, preferred_element_type=jnp.float32)
    cot_low = cotangent[0]
    d_activated = jnp.einsum("tc,fc->tf", cot_low, down_full, preferred_element_type=jnp.float32)
    unused_gelu, gelu_pull = jax.vjp(
        lambda values: jax.nn.gelu(values, approximate=False), up_values
    )
    d_up_low = gelu_pull(d_activated)[0].astype(jnp.bfloat16)
    d_second = jnp.einsum("tf,cf->tc", d_up_low, up_full, preferred_element_type=jnp.float32)
    unused_second, second_pull = jax.vjp(layer_norm, residual, second_gain, second_shift)
    d_norm_two, d_second_gain, d_second_shift = second_pull(d_second)
    d_residual = cot_low.astype(jnp.float32) + d_norm_two
    d_branch_low = d_residual.astype(jnp.bfloat16)
    d_attended_low = jnp.einsum(
        "tc,kc->tk", d_branch_low, out_full, preferred_element_type=jnp.float32
    ).astype(jnp.bfloat16)
    d_attended3 = d_attended_low.reshape(rows_here, head_count, head_width)
    row_dots = jnp.einsum("qhe,qhe->hq", d_attended3.astype(jnp.float32), attended)
    keys_all, values_all = (
        lax.all_gather(key_rows, "blk", axis=0, tiled=True),
        lax.all_gather(value_rows, "blk", axis=0, tiled=True),
    )
    length = keys_all.shape[0]
    step_rows = math.gcd(length, block_limit)

    def block_terms(block_index):
        block_start = block_index * step_rows
        key_block = lax.dynamic_slice_in_dim(keys_all, block_start, step_rows, 0).reshape(
            step_rows, head_count, head_width
        )
        value_block = lax.dynamic_slice_in_dim(values_all, block_start, step_rows, 0).reshape(
            step_rows, head_count, head_width
        )
        key_seg = segment_of(starts_row, block_start + jnp.arange(step_rows, dtype=jnp.int32))
        scores, allowed = scores_with_mask(queries, key_block, query_seg, key_seg)
        probability = jnp.where(allowed, jnp.exp(scores - log_total[:, :, None]), 0.0)
        d_probs = jnp.einsum(
            "qhe,khe->hqk", d_attended3, value_block, preferred_element_type=jnp.float32
        )
        d_scores = (probability * (d_probs - row_dots[:, :, None])).astype(jnp.bfloat16)
        return (key_block, probability, d_scores)

    dq_start = jnp.zeros((rows_here, head_count, head_width), jnp.float32)

    def back_block(dq_sum, block_index):
        key_block, probability, d_scores = block_terms(block_index)
        dq_sum = dq_sum + jnp.einsum(
            "hqk,khe->qhe", d_scores, key_block, preferred_element_type=jnp.float32
        )
        dk_block = (
            jnp.einsum("hqk,qhe->khe", d_scores, queries, preferred_element_type=jnp.float32)
            * score_scale
        )
        dv_block = jnp.einsum(
            "hqk,qhe->khe",
            probability.astype(jnp.bfloat16),
            d_attended3,
            preferred_element_type=jnp.float32,
        )
        return (
            dq_sum,
            (dk_block.reshape(step_rows, model_width), dv_block.reshape(step_rows, model_width)),
        )

    dq_sum, (dk_terms, dv_terms) = lax.scan(back_block, dq_start, jnp.arange(length // step_rows))
    dk_rows, dv_rows = (
        lax.psum_scatter(
            dk_terms.reshape(length, model_width).astype(jnp.bfloat16),
            "blk",
            scatter_dimension=0,
            tiled=True,
        ).astype(jnp.float32),
        lax.psum_scatter(
            dv_terms.reshape(length, model_width).astype(jnp.bfloat16),
            "blk",
            scatter_dimension=0,
            tiled=True,
        ).astype(jnp.float32),
    )
    d_packed = jnp.concatenate(
        [(dq_sum * score_scale).reshape(rows_here, model_width), dk_rows, dv_rows], axis=1
    ).astype(jnp.bfloat16)
    d_normed = jnp.einsum("tn,cn->tc", d_packed, qkv_full, preferred_element_type=jnp.float32)
    unused_first, first_pull = jax.vjp(layer_norm, inputs, first_gain, first_shift)
    d_norm_one, d_first_gain, d_first_shift = first_pull(d_normed)
    grad_hidden = d_residual + d_norm_one
    d_bias = jnp.sum(d_up_low, axis=0, dtype=jnp.float32)
    wide_share = lax.psum_scatter(
        jnp.concatenate(
            [
                jnp.einsum("tc,tn->cn", normed_low, d_packed, preferred_element_type=jnp.float32),
                jnp.einsum(
                    "tc,tn->cn", attended_low, d_branch_low, preferred_element_type=jnp.float32
                ),
                jnp.einsum("tc,tn->cn", second_low, d_up_low, preferred_element_type=jnp.float32),
            ],
            axis=1,
        ).astype(jnp.bfloat16),
        "rows",
        scatter_dimension=0,
        tiled=True,
    )
    down_share = lax.psum_scatter(
        jnp.einsum("tf,tn->fn", activated_low, cot_low, preferred_element_type=jnp.float32).astype(
            jnp.bfloat16
        ),
        "rows",
        scatter_dimension=0,
        tiled=True,
    )
    wide_grads, down_grads = (
        lax.psum(wide_share, "blk").astype(jnp.float32),
        lax.psum(down_share, "blk").astype(jnp.float32),
    )
    grad_qkv = wide_grads[:, : 3 * model_width]
    grad_out = wide_grads[:, 3 * model_width : 4 * model_width]
    grad_up = wide_grads[:, 4 * model_width :]
    small_grads = lax.psum(
        (d_first_gain, d_first_shift, d_second_gain, d_second_shift, d_bias), ("rows", "blk")
    )
    return (
        output[None],
        grad_hidden[None],
        grad_qkv,
        grad_out,
        grad_up,
        down_grads,
        small_grads[0],
        small_grads[1],
        small_grads[2],
        small_grads[3],
        small_grads[4],
    )


MESH = pl.DeviceIdType.MESH
ROWS_Z, ROWS_Y = 4, 2
PAIR = 128


def place_of():
    index = lax.axis_index("rows")
    return index // 4, lax.rem(index // 2, 2), lax.rem(index, 2)


def row_of(z, y, core):
    return (lax.rem(z + ROWS_Z, ROWS_Z) * ROWS_Y + y) * 2 + core


def aligned(index, step):
    return pl.ds(pl.multiple_of(index * step, step), step)


def dot_nt(left, right):
    return lax.dot_general(left, right, (((1,), (1,)), ((), ())), preferred_element_type=jnp.float32)


def dot_nn(left, right):
    return jnp.dot(left, right, preferred_element_type=jnp.float32)


def head_lanes(width):
    lane = lax.broadcasted_iota(jnp.int32, (1, width), 1)
    return (lane < HEAD_DIM, lane >= HEAD_DIM)


def greet(peers):
    barrier = pltpu.get_barrier_semaphore()
    for peer in peers:
        pl.semaphore_signal(barrier, inc=1, device_id=peer, device_id_type=MESH)
    pl.semaphore_wait(barrier, len(peers))


def neighbours():
    z, y, core = place_of()
    return [
        {"rows": row_of(z + 1, y, core)},
        {"rows": row_of(z + 2, y, core)},
        {"rows": row_of(z + 3, y, core)},
        {"rows": row_of(z, 1 - y, core)},
        {"rows": row_of(z, y, 1 - core)},
        {"blk": 1 - lax.axis_index("blk")},
    ]


def write_mask(starts_ref, mask_ref):
    blocks, step, length = mask_ref.shape

    def rows(i, carry):
        key_at = lax.broadcasted_iota(jnp.int32, (step, length), 0) + i * step
        query_at = lax.broadcasted_iota(jnp.int32, (step, length), 1)
        key_seg = jnp.zeros((step, length), jnp.int32)
        query_seg = jnp.zeros((step, length), jnp.int32)
        for cell in range(starts_ref.shape[1]):
            start = starts_ref[0, cell]
            key_seg += (key_at >= start).astype(jnp.int32)
            query_seg += (query_at >= start).astype(jnp.int32)
        mask_ref[i] = jnp.where(key_seg == query_seg, 0.0, masked_score).astype(mask_ref.dtype)
        return carry

    lax.fori_loop(0, blocks, rows, 0)


def forward_kernel(
    hidden, cot, starts, gain1, shift1, gain2, shift2, bias_in, q_in, o_own, u_in, d_in,
    q_all, o_all, u_all, d_all, dy_all, normed_t_out, packed_out, lse_out, att_t_out, resid_out,
    second_t_out, act_out, act_t_out, slope_out,
    hid_other, normed, wq, wo, wu, packed, mask, att_part, att_own, resid, second,
    act, act_t, slope, normed_t, att_t, second_t, lse, u_wide, u_own, bias,
    local_sem, send_sem, recv_sem, x_send, x_recv,
):
    bf16 = jnp.bfloat16
    z, y, core = place_of()
    me = row_of(z, y, core)
    piece = lax.axis_index("blk")
    other = 1 - piece
    own_rows, width = hidden.shape
    length = packed.shape[0]
    d_own = d_in.at[pl.ds(piece * d_all.shape[1], d_all.shape[1])]
    own = (q_all.at[me], o_own, u_own, d_own)
    gathered = (q_all, o_all, u_all, d_all)
    x_peer = {"blk": other}
    peers = neighbours()
    pairs = packed.shape[1] // (3 * PAIR)
    first_gain, first_shift, second_gain, second_shift = (
        ref[...].reshape(1, width) for ref in (gain1, shift1, gain2, shift2)
    )

    def local(src, dst, index):
        return pltpu.make_async_copy(src, dst, local_sem.at[index])

    def block(w, stage):
        if stage < 3:
            slot, peer = me, peers[stage]
        elif stage < 7:
            slot, peer = row_of(z - (stage - 3), y, core), peers[3]
        elif stage < 11:
            slot, peer = row_of(z - (stage - 7), y, core), peers[4]
        else:
            slot, peer = row_of(z - (stage - 11), 1 - y, core), peers[4]
        src = own[w] if stage in (0, 1, 2, 3, 7) else gathered[w].at[slot]
        index = w * 15 + stage
        return pltpu.make_async_remote_copy(
            src_ref=src, dst_ref=gathered[w].at[slot], send_sem=send_sem.at[index],
            recv_sem=recv_sem.at[index], device_id=peer, device_id_type=MESH,
        )

    def start(w, *stages):
        for stage in stages:
            block(w, stage).start()

    def arrived(w, *stages):
        for stage in stages:
            block(w, stage).wait_recv()

    def to_x(src, dst, index):
        return pltpu.make_async_remote_copy(
            src_ref=src, dst_ref=dst, send_sem=x_send.at[index], recv_sem=x_recv.at[index],
            device_id=x_peer, device_id_type=MESH,
        )

    def relay_z(w, k):
        arrived(w, k - 1)
        start(w, 3 + k, 7 + k)

    def relay_y(w, k):
        arrived(w, 3 + k)
        start(w, 11 + k)

    third = q_in.shape[1] // 3
    share = third // 2
    q_picks = []
    for part in range(3):
        picked = q_in.at[:, pl.ds(pl.multiple_of(part * third + piece * share, 128), share)]
        q_picks.append(local(picked, q_all.at[me, :, pl.ds(part * share, share)], 17 + part))
        q_picks[-1].start()
    local(u_in, u_wide, 2).start()
    greet(peers)
    for copy in q_picks:
        copy.wait()
    start(0, 0, 2, 1)
    start(0, 3, 7)
    start(1, 0, 2, 1)
    start(1, 7)
    hidden_x = to_x(hidden, hid_other, 0)
    hidden_x.start()
    cot_x = to_x(cot, dy_all.at[piece], 1)
    cot_x.start()
    local(o_own, o_all.at[me], 1).start()
    local(d_own, d_all.at[me], 3).start()
    local(cot, dy_all.at[piece], 4).start()

    def norm_rows(read, half):
        step = 64

        def body(i, carry):
            rows = read(aligned(i, step)).astype(jnp.float32)
            low = layer_norm(rows, first_gain, first_shift).astype(bf16)
            normed[pl.ds(pl.multiple_of(half * own_rows + i * step, step), step), :] = low
            return carry

        lax.fori_loop(0, own_rows // step, body, 0)

    units_each = d_all.shape[1]
    group = 8 * units_each

    def mine(block):
        wide = block.astype(jnp.float32)
        halves = []
        for half in range(2):
            at = [slice((2 * j + half) * units_each, (2 * j + half + 1) * units_each) for j in range(4)]
            halves.append(jnp.concatenate([wide[:, cols] for cols in at], axis=1))
        return jnp.where(piece == 0, halves[0], halves[1])

    local(u_in, u_wide, 2).wait()
    for g in range(u_own.shape[1] // (group // 2)):
        cols = slice(g * group // 2, (g + 1) * group // 2)
        u_own[:, cols] = mine(u_wide[:, g * group : (g + 1) * group]).astype(bf16)
        bias[:, cols] = mine(bias_in[g * group : (g + 1) * group].reshape(1, group))
    start(2, 0, 2, 1)
    start(2, 7)
    start(3, 0, 2, 1)
    start(3, 7)
    local(u_own, u_all.at[me], 2).start()
    norm_rows(lambda rows: hidden[rows, :], piece)
    relay_z(0, 1)
    relay_z(0, 3)
    start(1, 3)
    write_mask(starts, mask)
    relay_y(0, 0)
    relay_y(0, 1)
    hidden_x.wait_recv()
    norm_rows(lambda rows: hid_other[rows, :], other)
    relay_z(0, 2)
    relay_y(0, 3)

    def flip(i, carry):
        normed_t[aligned(i, 128), :] = normed[:, aligned(i, 128)].T
        return carry

    lax.fori_loop(0, width // 128, flip, 0)
    local(normed_t, normed_t_out, 8).start()
    relay_z(1, 1)
    relay_y(0, 2)
    relay_z(1, 3)
    start(2, 3)
    arrived(0, *range(7, 15))
    local(q_all, wq, 5).start()
    local(q_all, wq, 5).wait()

    column = lax.broadcasted_iota(jnp.int32, (1, 3 * PAIR), 1)

    def project(i, carry):
        cols = aligned(i, 3 * PAIR)
        weight = wq[:, :, cols].reshape(width, 3 * PAIR)
        value = dot_nn(normed[...], weight).astype(bf16)
        factor = jnp.where(i * 3 * PAIR + column < share, HEAD_DIM ** (-0.5), 1.0).astype(bf16)
        packed[:, cols] = value * factor
        return carry

    lax.fori_loop(0, pairs, project, 0)
    local(packed, packed_out, 9).start()
    first_lanes = head_lanes(PAIR)

    def attend(p):
        at_q, at_k, at_v = (slice(t * share + PAIR * p, t * share + PAIR * (p + 1)) for t in range(3))
        value_t = packed[:, at_v].T
        step = 256

        def rows(i, carry):
            queries = packed[aligned(i, step), at_q]
            keys = packed[:, at_k]
            halves = []
            for h in range(2):
                one = jnp.where(first_lanes[h], queries, jnp.zeros_like(queries))
                scores = dot_nt(keys, one) + mask[:, :, aligned(i, step)].reshape(length, step)
                top = jnp.max(scores, axis=0, keepdims=True)
                weights = jnp.exp(scores - top)
                total = jnp.sum(weights, axis=0, keepdims=True)
                lse[2 * p + h : 2 * p + h + 1, aligned(i, step)] = top + jnp.log(total)
                summed = dot_nn(value_t[h * HEAD_DIM : (h + 1) * HEAD_DIM], weights.astype(bf16))
                halves.append(summed / total)
            both = jnp.concatenate(halves, axis=0).T.astype(bf16)
            att_part[aligned(i, step), p * PAIR : (p + 1) * PAIR] = both
            return carry

        lax.fori_loop(0, length // step, rows, 0)

    def att_cols(half, p):
        return pl.ds(pl.multiple_of(half * pairs * PAIR + p * PAIR, PAIR), PAIR)

    att_x = []
    for p in range(pairs):
        attend(p)
        part = att_part.at[pl.ds(pl.multiple_of(other * own_rows, 128), own_rows), pl.ds(p * PAIR, PAIR)]
        att_x.append(to_x(part, att_own.at[:, att_cols(piece, p)], 2 + p))
        att_x[-1].start()
        mine = att_part[pl.ds(pl.multiple_of(piece * own_rows, 128), own_rows), p * PAIR : (p + 1) * PAIR]
        att_own[:, att_cols(piece, p)] = mine
        if p == 0:
            relay_y(1, 0)
            relay_y(1, 1)
        elif p == 1:
            relay_z(1, 2)
        elif p == 2:
            relay_y(1, 3)
        elif p == 3:
            relay_z(2, 1)
        elif p == 4:
            relay_y(1, 2)
    local(lse, lse_out, 10).start()
    for copy in att_x:
        copy.wait_recv()
    arrived(1, *range(7, 15))
    local(own[1], gathered[1].at[me], 1).wait()
    local(o_all, wo, 6).start()

    def flip_att(i, carry):
        att_t[aligned(i, 128), :] = att_own[:, aligned(i, 128)].T
        return carry

    lax.fori_loop(0, width // 128, flip_att, 0)
    local(att_t, att_t_out, 11).start()
    relay_z(2, 3)
    start(3, 3)
    local(o_all, wo, 6).wait()

    def merge(i, carry):
        cols = aligned(i, 256)
        weight = wo[:, :, cols].reshape(width, 256)
        resid[:, cols] = hidden[:, cols].astype(jnp.float32) + dot_nn(att_own[...], weight)
        return carry

    lax.fori_loop(0, width // 256, merge, 0)
    local(resid, resid_out, 12).start()

    def second_rows(i, carry):
        rows = aligned(i, 64)
        second[piece, rows, :] = layer_norm(resid[rows, :], second_gain, second_shift).astype(bf16)
        return carry

    lax.fori_loop(0, own_rows // 64, second_rows, 0)
    second_x = to_x(second.at[piece], second.at[piece], 2 + pairs)
    second_x.start()
    relay_y(2, 0)
    relay_y(2, 1)
    relay_z(2, 2)
    second_x.wait_recv()

    def flip_second(i, carry):
        cols = aligned(i, 128)
        second_t[cols, :] = second[:, :, cols].reshape(length, 128).T
        return carry

    lax.fori_loop(0, width // 128, flip_second, 0)
    local(second_t, second_t_out, 13).start()
    relay_y(2, 3)
    relay_z(3, 1)
    relay_y(2, 2)
    arrived(2, *range(7, 15))
    local(own[2], gathered[2].at[me], 2).wait()
    local(u_all, wu, 7).start()
    local(u_all, wu, 7).wait()
    relay_z(3, 3)
    unit = 256
    steps = act.shape[1] // unit

    def expand(i, carry):
        cols = aligned(i // 2, unit)
        rows = aligned(lax.rem(i, 2), own_rows)
        weight = wu[:, :, cols].reshape(width, unit)
        up = dot_nn(second[lax.rem(i, 2)], weight) + bias[:, cols]
        cdf = 0.5 * (1.0 + lax.erf(up * (0.5 ** 0.5)))
        pdf = jnp.exp(up * up * -0.5) * ((2.0 * math.pi) ** -0.5)
        value = (up * cdf).astype(bf16)
        act[rows, cols] = value
        act_t[cols, rows] = value.T
        slope[rows, cols] = (cdf + up * pdf).astype(bf16)
        return carry

    lax.fori_loop(0, steps, expand, 0)
    relay_y(3, 0)
    relay_y(3, 1)
    lax.fori_loop(steps, 2 * steps, expand, 0)
    local(act, act_out, 14).start()
    local(act_t, act_t_out, 15).start()
    local(slope, slope_out, 16).start()
    relay_z(3, 2)
    relay_y(3, 3)
    relay_y(3, 2)
    arrived(3, *range(7, 15))
    cot_x.wait_recv()
    local(own[3], gathered[3].at[me], 3).wait()
    local(cot, dy_all.at[piece], 4).wait()
    local(normed_t, normed_t_out, 8).wait()
    local(packed, packed_out, 9).wait()
    local(lse, lse_out, 10).wait()
    local(att_t, att_t_out, 11).wait()
    local(resid, resid_out, 12).wait()
    local(second_t, second_t_out, 13).wait()
    local(act, act_out, 14).wait()
    local(act_t, act_t_out, 15).wait()
    local(slope, slope_out, 16).wait()
    for w in range(4):
        for stage in range(15):
            block(w, stage).wait_send()
    for copy in [hidden_x, cot_x, second_x] + att_x:
        copy.wait_send()


def forward(hidden, cot, starts, gain1, shift1, gain2, shift2, bias, qkv, out, up, down):
    own_rows, width = hidden.shape
    length = 2 * own_rows
    cols = qkv.shape[1] // 2
    units = up.shape[1] // 2
    rows = up.shape[0]
    bf16, f32 = jnp.bfloat16, jnp.float32
    shards = lax.axis_size("rows")
    head_rows = 16
    outs = [
        ((shards, rows, cols), bf16),
        ((shards, rows, width), bf16),
        ((shards, rows, units), bf16),
        ((shards, down.shape[0] // 2, width), bf16),
        ((2, own_rows, width), bf16),
        ((width, length), bf16),
        ((length, cols), bf16),
        ((head_rows, length), f32),
        ((width, own_rows), bf16),
        ((own_rows, width), f32),
        ((width, length), bf16),
        ((length, units), bf16),
        ((units, length), bf16),
        ((length, units), bf16),
    ]
    scratch = [
        ((own_rows, width), bf16),
        ((length, width), bf16),
        ((shards, rows, cols), bf16),
        ((shards, rows, width), bf16),
        ((shards, rows, units), bf16),
        ((length, cols), bf16),
        ((length // 48, 48, length), f32),
        ((length, cols // 3), bf16),
        ((own_rows, width), bf16),
        ((own_rows, width), f32),
        ((2, own_rows, width), bf16),
        ((length, units), bf16),
        ((units, length), bf16),
        ((length, units), bf16),
        ((width, length), bf16),
        ((width, own_rows), bf16),
        ((width, length), bf16),
        ((head_rows, length), f32),
        ((rows, 2 * units), bf16),
        ((rows, units), bf16),
        ((1, units), f32),
    ]
    vmem = pl.BlockSpec(memory_space=pltpu.VMEM)
    anywhere = pl.BlockSpec(memory_space=pl.ANY)
    smem = pl.BlockSpec(memory_space=pltpu.SMEM)
    dma = pltpu.SemaphoreType.DMA
    x_copies = 3 + cols // (3 * PAIR)
    return pl.pallas_call(
        forward_kernel,
        out_shape=[jax.ShapeDtypeStruct(shape, kind) for shape, kind in outs],
        in_specs=[vmem, anywhere, smem] + [vmem] * 5 + [anywhere] * 4,
        out_specs=[anywhere] * len(outs),
        scratch_shapes=[pltpu.VMEM(shape, kind) for shape, kind in scratch]
        + [dma((20,)), dma((60,)), dma((60,)), dma((x_copies,)), dma((x_copies,))],
        compiler_params=pltpu.CompilerParams(
            collective_id=1, has_side_effects=True, vmem_limit_bytes=60 * 1024 * 1024
        ),
        name="forward",
    )(hidden, cot, starts, gain1, shift1, gain2, shift2, bias, qkv, out, up, down)


UNIT = 640
SLOTS = 2


def norm_back(values, gain, grad):
    centred = values - jnp.mean(values, axis=-1, keepdims=True)
    scale = lax.rsqrt(jnp.mean(centred * centred, axis=-1, keepdims=True) + 1e-05)
    unit = centred * scale
    scaled = grad * gain
    mean_one = jnp.mean(scaled, axis=-1, keepdims=True)
    mean_two = jnp.mean(scaled * unit, axis=-1, keepdims=True)
    d_values = scale * (scaled - mean_one - unit * mean_two)
    d_gain = jnp.sum(grad * unit, axis=0, keepdims=True)
    d_shift = jnp.sum(grad, axis=0, keepdims=True)
    return d_values, d_gain, d_shift


def backward_kernel(
    starts, gain1, gain2, hidden, dy_all, q_all, o_all, u_all, d_all, normed_t, packed, lse_in, att_t,
    resid, second_t, act, act_t, slope,
    output, grad_hidden, units_out, pairs_out, small_out,
    lhs, half_act, wide, wd, wu, dy, first, second, d_att, x_in0, x_in1, x_out0, x_out1,
    down_own, parts, core_in, core_in_q, y_in, y_in_q, z_in, z_in_q, lse, acc_k, acc_v,
    bias_sum, small, small_core, small_y, small_z,
    local_sem, a_send, a_recv, b_send, b_recv, c_send, c_recv, g_send, g_recv, x_send, x_recv,
    s_send, s_recv, keep_sem,
):
    bf16, f32 = jnp.bfloat16, jnp.float32
    z, y, core = place_of()
    piece = lax.axis_index("blk")
    other = 1 - piece
    own_rows, width = first.shape
    length = 2 * own_rows
    branch = half_act.at[:, pl.ds(0, width)]
    units = wide.shape[1]
    cols = 3 * d_att.shape[1]
    pairs = d_att.shape[1] // PAIR
    peers = neighbours()
    wide_chunks = core_in.shape[0]
    first_gain, second_gain = gain1[...].reshape(1, width), gain2[...].reshape(1, width)
    half_rows = lambda half: pl.ds(pl.multiple_of(half * own_rows, 128), own_rows)

    def remote(src, dst, sends, recvs, index, peer):
        return pltpu.make_async_remote_copy(
            src_ref=src, dst_ref=dst, send_sem=sends.at[index], recv_sem=recvs.at[index],
            device_id=peer, device_id_type=MESH,
        )

    loads = {
        "act_t": (act_t, lhs, 0),
        "dy": (dy_all, dy, 1),
        "down": (d_all, wd, 2),
        "slope": (slope, wide, 3),
        "up": (u_all, wu, 4),
        "act_other": (act.at[half_rows(other)], half_act, 5),
        "act_own": (act.at[half_rows(piece)], half_act, 6),
        "resid": (resid, second, 7),
        "lse": (lse_in, lse, 8),
        "second_t": (second_t, lhs.at[:, pl.ds(0, lhs.shape[1] // 2)], 9),
        "att_t": (att_t, lhs.at[:, pl.ds(lhs.shape[1] // 2, lhs.shape[1] // 2), pl.ds(0, own_rows)], 10),
        "out": (o_all, wd.at[pl.ds(0, width)], 11),
        "normed_t": (normed_t, wd.at[pl.ds(width, width), pl.ds(0, length)], 12),
        "qkv": (q_all, wu.at[:, pl.ds(0, cols)], 13),
        "packed": (packed, wide.at[:, pl.ds(0, cols)], 14),
        "hidden": (hidden, branch, 15),
        "output": (second, output, 16),
        "grad_hidden": (first, grad_hidden, 17),
    }

    def local(name):
        src, dst, index = loads[name]
        return pltpu.make_async_copy(src, dst, local_sem.at[index])

    def buffers(i):
        if i < wide_chunks:
            return core_in.at[i], y_in.at[i], z_in.at[i], z_in.at[i, 0], units_out.at[:, i], UNIT
        i -= wide_chunks
        return core_in_q.at[i], y_in_q.at[i], z_in_q.at[i], z_in_q.at[i, 0], pairs_out.at[:, i], 3 * PAIR

    def copy_a(i):
        into, _, _, _, _, n = buffers(i)
        return remote(parts.at[i % SLOTS, 1 - core, :, :, :, pl.ds(0, n)], into, a_send, a_recv, i, peers[4])

    def copy_b(i):
        sums, into, _, _, _, _ = buffers(i)
        return remote(sums.at[1 - y], into, b_send, b_recv, i, peers[3])

    def copy_c(i, k):
        _, sums, into, _, _, _ = buffers(i)
        return remote(sums.at[lax.rem(z + k, ROWS_Z)], into.at[k - 1], c_send, c_recv, 3 * i + k - 1, peers[k - 1])

    def copy_g(i):
        _, _, _, share, out, _ = buffers(i)
        return remote(share, out.at[piece], g_send, g_recv, i, peers[5])

    def keep_g(i):
        _, _, _, share, out, _ = buffers(i)
        return pltpu.make_async_copy(share, out.at[piece], keep_sem.at[i])

    def finish_a(i):
        sums, _, _, _, _, n = buffers(i)
        copy_a(i).wait_recv()
        slot = i % SLOTS
        sums[1 - y] += parts[slot, core, 1 - y, :, :, :n]
        copy_b(i).start()
        sums[y] += parts[slot, core, y, :, :, :n]
        copy_a(i).wait_send()

    def finish_b(i):
        mine, sums, _, _, _, _ = buffers(i)
        copy_b(i).wait_recv()
        sums[...] += mine[y]
        for k in (1, 3, 2):
            copy_c(i, k).start()

    def finish_c(i):
        _, sums, terms, share, _, _ = buffers(i)
        for k in (1, 3, 2):
            copy_c(i, k).wait_recv()
        total = sums[z].astype(f32)
        for k in range(3):
            total += terms[k].astype(f32)
        share[...] = total.astype(bf16)
        copy_g(i).start()
        keep_g(i).start()

    def grad_chunk(i, left, right):
        slot = i % SLOTS

        def one_z(to_z, carry):
            value = dot_nn(left(to_z), right()).astype(bf16)
            n = value.shape[1]
            rows = value.shape[0] // 4
            for block in range(4):
                to_y, to_core = divmod(block, 2)
                parts[slot, to_core, to_y, to_z, :, :n] = value[block * rows : (block + 1) * rows]
            return carry

        lax.fori_loop(0, ROWS_Z, one_z, 0)
        copy_a(i).start()

    for name in ("act_t", "dy", "down", "slope", "act_other", "up", "resid", "lse"):
        local(name).start()
    greet(peers)
    local("act_t").wait()
    local("dy").wait()
    block_rows = parts.shape[4]

    def grad_down(i):
        h, column = divmod(i, 2)

        def left(to_z):
            rows = lhs[pl.ds(to_z * 4, 4), h * block_rows : (h + 1) * block_rows, :]
            return rows.reshape(4 * block_rows, length)

        grad_chunk(i, left, lambda: dy[:, :, column * UNIT : (column + 1) * UNIT].reshape(length, UNIT))

    grad_down(0)
    grad_down(1)
    finish_a(0)
    grad_down(2)
    finish_a(1)
    grad_down(3)
    local("second_t").start()
    local("att_t").start()
    local("down").wait()
    local("slope").wait()

    tile = 256

    def d_units(i, carry):
        at = aligned(i, tile)
        sums = jnp.zeros((1, tile), f32)
        for half in range(2):
            rows = slice(half * own_rows, (half + 1) * own_rows)
            value = dot_nt(dy[half], wd[at, :]) * wide[rows, at].astype(f32)
            low = value.astype(bf16)
            wide[rows, at] = low
            sums += jnp.sum(low.astype(f32), axis=0, keepdims=True)
        bias_sum[:, at] = sums
        return carry

    lax.fori_loop(0, 4, d_units, 0)
    finish_a(2)
    finish_a(3)
    lax.fori_loop(4, units // tile, d_units, 0)
    local("up").wait()

    def d_second(half, write):
        def body(i, carry):
            at = aligned(i, tile)
            write(at, dot_nt(wide[half_rows(half), :], wu[at, :]))
            return carry

        lax.fori_loop(0, width // tile, body, 0)

    def write_out0(at, value):
        x_out0[:, at] = value.astype(bf16)

    def write_first(at, value):
        first[:, at] = value

    d_second(other, write_out0)
    second_x = remote(x_out0, x_in0, x_send, x_recv, 0, peers[5])
    second_x.start()
    d_second(piece, write_first)
    local("qkv").start()
    finish_b(0)
    local("act_other").wait()

    def down_part(target):
        def body(i, carry):
            at = aligned(i, tile)
            target[:, at] = dot_nn(half_act[...], wd[:, at]).astype(bf16)
            return carry

        lax.fori_loop(0, width // tile, body, 0)

    down_part(x_out1)
    local("act_own").start()
    local("second_t").wait()

    def grad_up(i):
        def left(to_z):
            rows = lhs[pl.ds(to_z * 4, 4), :block_rows, :]
            return rows.reshape(4 * block_rows, length)

        grad_chunk(4 + i, left, lambda: wide[:, i * UNIT : (i + 1) * UNIT])

    grad_up(0)
    grad_up(1)
    local("act_own").wait()
    finish_a(4)
    finish_b(1)
    down_part(down_own)
    local("out").start()
    local("normed_t").start()
    finish_a(5)
    grad_up(2)
    grad_up(3)
    local("packed").start()
    mask = lhs.at[:, pl.ds(0, length // lhs.shape[0]), :]
    write_mask(starts, mask)
    finish_a(6)
    finish_a(7)
    finish_c(0)
    finish_b(2)
    local("resid").wait()
    second_x.wait_recv()
    step = 64

    def back_two(i, carry):
        rows = aligned(i, step)
        grad = first[rows, :] + x_in0[rows, :].astype(f32)
        d_values, d_gain, d_shift = norm_back(second[rows, :], second_gain, grad)
        total = dy[piece, rows, :].astype(f32) + d_values
        first[rows, :] = total
        branch[rows, :] = total.astype(bf16)
        return carry[0] + d_gain, carry[1] + d_shift

    zeros = jnp.zeros((1, width), f32)
    gain_two, shift_two = lax.fori_loop(0, own_rows // step, back_two, (zeros, zeros))
    small[2:3, :] = gain_two
    small[3:4, :] = shift_two
    local("out").wait()
    second_x.wait_send()
    d_width = d_att.shape[1]

    def d_attended(half):
        rows = pl.ds(pl.multiple_of(half * d_width, 128), d_width)
        return dot_nt(branch[...], wd[rows, :]).astype(bf16)

    x_out0[:, :d_width] = d_attended(other)
    att_x = remote(x_out0.at[:, pl.ds(0, d_width)], d_att.at[half_rows(piece)], x_send, x_recv, 1, peers[5])
    att_x.start()
    down_x = remote(x_out1, x_in1, x_send, x_recv, 2, peers[5])
    down_x.start()
    d_att[half_rows(piece), :] = d_attended(piece)
    local("att_t").wait()

    def grad_out(i):
        def left(to_z):
            rows = lhs[pl.ds(to_z * 4, 4), block_rows : 2 * block_rows, :own_rows]
            return rows.reshape(4 * block_rows, own_rows)

        grad_chunk(8 + i, left, lambda: branch[:, i * UNIT : (i + 1) * UNIT])

    grad_out(0)
    grad_out(1)
    finish_c(1)
    finish_b(3)
    finish_a(8)
    finish_a(9)
    local("hidden").start()
    local("lse").wait()
    local("packed").wait()
    local("normed_t").wait()
    att_x.wait_recv()
    first_lanes = head_lanes(PAIR)

    def pair_cols(p):
        return tuple(slice(t * d_width + PAIR * p, t * d_width + PAIR * (p + 1)) for t in range(3))

    def attend_back(p):
        at_q, at_k, at_v = pair_cols(p)
        keys_t = wide[:, at_k].T
        acc_k[...] = jnp.zeros_like(acc_k)
        acc_v[...] = jnp.zeros_like(acc_v)
        chunk = 256

        def body(i, carry):
            rows = aligned(i, chunk)
            keys = wide[:, at_k]
            values = wide[:, at_v]
            queries = wide[rows, at_q]
            grads = d_att[rows, p * PAIR : (p + 1) * PAIR]
            blocked = mask[:, :, rows].reshape(length, chunk).astype(f32)
            parts_q = []
            for h in range(2):
                one_q = jnp.where(first_lanes[h], queries, jnp.zeros_like(queries))
                one_g = jnp.where(first_lanes[h], grads, jnp.zeros_like(grads))
                scores = dot_nt(keys, one_q) + (blocked - lse[2 * p + h : 2 * p + h + 1, rows])
                probs = jnp.exp(scores)
                d_probs = dot_nt(values, one_g)
                dots = jnp.sum(probs * d_probs, axis=0, keepdims=True)
                d_scores = (probs * (d_probs - dots)).astype(bf16)
                acc_v[...] += dot_nn(probs.astype(bf16), one_g)
                acc_k[...] += dot_nn(d_scores, one_q)
                parts_q.append(dot_nn(keys_t[h * HEAD_DIM : (h + 1) * HEAD_DIM], d_scores))
            d_queries = jnp.concatenate(parts_q, axis=0).T * HEAD_DIM ** (-0.5)
            wide[rows, at_q] = d_queries.astype(bf16)
            return carry

        lax.fori_loop(0, length // chunk, body, 0)
        wide[:, at_k] = acc_k[...].astype(bf16)
        wide[:, at_v] = acc_v[...].astype(bf16)

    def grad_pair(p):
        def left(to_z):
            return wd[pl.ds(pl.multiple_of(width + to_z * 4 * block_rows, 64), 4 * block_rows), :length]

        grad_chunk(10 + p, left, lambda: jnp.concatenate([wide[:, at] for at in pair_cols(p)], axis=1))

    def write_output():
        down_x.wait_recv()

        def body(i, carry):
            rows = aligned(i, step)
            second[rows, :] += down_own[rows, :].astype(f32) + x_in1[rows, :].astype(f32)
            return carry

        lax.fori_loop(0, own_rows // step, body, 0)
        local("output").start()

    ticks = {
        0: lambda: (finish_c(2), finish_b(4)),
        1: lambda: (finish_a(10), finish_c(3), finish_b(5)),
        2: lambda: (finish_a(11), finish_c(4), finish_b(6)),
        3: lambda: (finish_a(12), write_output(), finish_c(5), finish_b(7)),
        4: lambda: (finish_a(13), finish_c(6)),
    }
    for p in range(pairs):
        attend_back(p)
        grad_pair(p)
        ticks[p]()
    finish_a(14)
    local("qkv").wait()
    local("output").wait()
    att_x.wait_send()

    def d_normed(half, write):
        def body(i, carry):
            at = aligned(i, tile)
            write(at, dot_nt(wide[half_rows(half), :cols], wu[at, :cols]))
            return carry

        lax.fori_loop(0, width // tile, body, 0)

    def write_second(at, value):
        second[:, at] = value

    d_normed(other, write_out0)
    normed_x = remote(x_out0, x_in0, x_send, x_recv, 3, peers[5])
    normed_x.start()
    finish_b(8)
    d_normed(piece, write_second)
    finish_c(7)
    finish_b(9)
    local("hidden").wait()
    finish_c(8)
    finish_b(10)
    normed_x.wait_recv()

    def back_one(i, carry):
        rows = aligned(i, step)
        grad = second[rows, :] + x_in0[rows, :].astype(f32)
        d_values, d_gain, d_shift = norm_back(branch[rows, :].astype(f32), first_gain, grad)
        first[rows, :] += d_values
        return carry[0] + d_gain, carry[1] + d_shift

    gain_one, shift_one = lax.fori_loop(0, own_rows // step, back_one, (zeros, zeros))
    local("grad_hidden").start()
    small[0:1, :] = gain_one
    small[1:2, :] = shift_one
    small[4:5, :] = bias_sum[:, :width]
    small[5:6, :] = bias_sum[:, width:]
    small[6:8, :] = jnp.zeros((2, width), f32)
    core_x = remote(small, small_core, s_send, s_recv, 0, peers[4])
    core_x.start()
    finish_b(11)
    core_x.wait()
    small[...] += small_core[...]
    y_x = remote(small, small_y, s_send, s_recv, 1, peers[3])
    y_x.start()
    finish_c(9)
    finish_b(12)
    finish_c(10)
    finish_b(13)
    finish_c(11)
    finish_b(14)
    y_x.wait()
    small_z[z] = small[...] + small_y[...]
    z_x = [remote(small_z.at[z], small_z.at[z], s_send, s_recv, 1 + k, peers[k - 1]) for k in (1, 2, 3)]
    for copy in z_x:
        copy.start()
    finish_c(12)
    finish_c(13)
    for copy in z_x:
        copy.wait()
    small[...] = ((small_z[0] + small_z[1]) + small_z[2]) + small_z[3]
    share_x = remote(small, small_out.at[piece], s_send, s_recv, 5, peers[5])
    share_x.start()
    share_keep = pltpu.make_async_copy(small, small_out.at[piece], keep_sem.at[15])
    share_keep.start()
    finish_c(14)
    for i in range(15):
        copy_b(i).wait_send()
        for k in (1, 2, 3):
            copy_c(i, k).wait_send()
        copy_g(i).wait()
        keep_g(i).wait()
    share_x.wait()
    share_keep.wait()
    down_x.wait_send()
    normed_x.wait_send()
    local("grad_hidden").wait()


def backward(starts, gain1, gain2, hidden, dy_all, q_all, o_all, u_all, d_all, *kept):
    bf16, f32 = jnp.bfloat16, jnp.float32
    _, own_rows, width = dy_all.shape
    length = 2 * own_rows
    cols, units = q_all.shape[1], u_all.shape[1]
    rows = width // 16
    wide_units, pairs = 10, cols // (3 * PAIR)
    pair_cols = 3 * PAIR
    outs = [
        ((own_rows, width), f32),
        ((own_rows, width), f32),
        ((2, wide_units, rows, UNIT), bf16),
        ((2, pairs, rows, pair_cols), bf16),
        ((2, 8, width), f32),
    ]
    token = ((own_rows, width), bf16)
    scratch = [
        ((16, 2 * rows, length), bf16),
        ((own_rows, units), bf16),
        ((length, units), bf16),
        ((units, width), bf16),
        ((width, units), bf16),
        ((2, own_rows, width), bf16),
        ((own_rows, width), f32),
        ((own_rows, width), f32),
        ((length, cols // 3), bf16),
        token, token, token, token, token,
        ((SLOTS, 2, 2, ROWS_Z, rows, UNIT), bf16),
        ((wide_units, 2, ROWS_Z, rows, UNIT), bf16),
        ((pairs, 2, ROWS_Z, rows, pair_cols), bf16),
        ((wide_units, ROWS_Z, rows, UNIT), bf16),
        ((pairs, ROWS_Z, rows, pair_cols), bf16),
        ((wide_units, 3, rows, UNIT), bf16),
        ((pairs, 3, rows, pair_cols), bf16),
        ((16, length), f32),
        ((length, PAIR), f32),
        ((length, PAIR), f32),
        ((1, units), f32),
        ((8, width), f32),
        ((8, width), f32),
        ((8, width), f32),
        ((ROWS_Z, 8, width), f32),
    ]
    vmem = pl.BlockSpec(memory_space=pltpu.VMEM)
    anywhere = pl.BlockSpec(memory_space=pl.ANY)
    smem = pl.BlockSpec(memory_space=pltpu.SMEM)
    chunks = wide_units + pairs
    dma = lambda n: pltpu.SemaphoreType.DMA((n,))
    sems = [18] + [chunks] * 4 + [3 * chunks] * 2 + [chunks] * 2 + [4, 4, 6, 6, chunks + 1]
    return pl.pallas_call(
        backward_kernel,
        out_shape=[jax.ShapeDtypeStruct(shape, kind) for shape, kind in outs],
        in_specs=[smem, vmem, vmem] + [anywhere] * (6 + len(kept)),
        out_specs=[anywhere] * len(outs),
        scratch_shapes=[pltpu.VMEM(shape, kind) for shape, kind in scratch] + [dma(n) for n in sems],
        compiler_params=pltpu.CompilerParams(
            collective_id=2, has_side_effects=True, vmem_limit_bytes=60 * 1024 * 1024
        ),
        name="backward",
    )(starts, gain1, gain2, hidden, dy_all, q_all, o_all, u_all, d_all, *kept)


def finish_kernel(
    raw_output, raw_grad, units_lo, units_hi, pairs_in, small,
    output, grad_hidden, qkv, out, up, down, gain1, shift1, gain2, shift2, bias,
):
    f32 = jnp.float32
    step = pl.program_id(0)
    output[0] = raw_output[...]
    grad_hidden[0] = raw_grad[...]
    rows = out.shape[0]
    width = small.shape[2]
    units_in = (units_lo, units_hi)

    def mixed(first, second):
        each = first.shape[1] // 4
        blocks = []
        for j in range(4):
            at = slice(j * each, (j + 1) * each)
            blocks += [first[:, at].astype(f32), second[:, at].astype(f32)]
        return jnp.concatenate(blocks, axis=1)

    for now in range(2):

        @pl.when(step == now)
        def _():
            for i in range(4):
                h, column = divmod(i, 2)
                at = slice(column * UNIT, (column + 1) * UNIT)
                down[h * rows : (h + 1) * rows, at] = units_in[now][0, i].astype(f32)
            for i in range(2):
                chunk = 4 + 2 * now + i
                at = slice(i * 2 * UNIT, (i + 1) * 2 * UNIT)
                up[:, at] = mixed(units_lo[0, chunk], units_hi[0, chunk])
            out[...] = units_lo[0, 8 + now].astype(f32) + units_hi[0, 8 + now].astype(f32)
            pairs = pairs_in.shape[1]
            for block in range(3 * now, 3 * now + 3):
                part, piece = divmod(block, 2)
                for p in range(pairs):
                    at = (block - 3 * now) * pairs * PAIR + p * PAIR
                    chunk = pairs_in[piece, p, :, part * PAIR : (part + 1) * PAIR]
                    qkv[:, at : at + PAIR] = chunk.astype(f32)

    @pl.when(step == 0)
    def _():
        for i, ref in enumerate((gain1, shift1, gain2, shift2)):
            ref[...] = (small[0, i : i + 1, :] + small[1, i : i + 1, :]).reshape(width)
        for g in range(2):
            for j in range(2):
                at = slice(j * UNIT, (j + 1) * UNIT)
                lo, hi = small[0, 4 + g : 5 + g, at], small[1, 4 + g : 5 + g, at]
                begin = (2 * g + j) * 2 * UNIT
                bias[begin : begin + 2 * UNIT] = mixed(lo, hi).reshape(2 * UNIT)


def finish(raw_output, raw_grad, units_in, pairs_in, small):
    f32 = jnp.float32
    own_rows, width = raw_output.shape
    rows = units_in.shape[2]
    shapes = [
        (1, own_rows, width), (1, own_rows, width), (rows, 3 * width), (rows, width), (rows, 8 * UNIT),
        (4 * rows, width), (width,), (width,), (width,), (width,), (8 * UNIT,),
    ]
    token = pl.BlockSpec((own_rows // 2, width), lambda s: (s, 0))
    token_out = pl.BlockSpec((1, own_rows // 2, width), lambda s: (0, s, 0))
    columns = lambda n: pl.BlockSpec((rows, n // 2), lambda s: (0, s))
    fixed = lambda shape: pl.BlockSpec(shape, lambda s: (0,) * len(shape))
    half = lambda i: pl.BlockSpec((1,) + units_in.shape[1:], lambda s: (i, 0, 0, 0))
    return pl.pallas_call(
        finish_kernel,
        grid=(2,),
        out_shape=[jax.ShapeDtypeStruct(shape, f32) for shape in shapes],
        in_specs=[token, token, half(0), half(1), fixed(pairs_in.shape), fixed(small.shape)],
        out_specs=[
            token_out, token_out, columns(3 * width), columns(width), columns(8 * UNIT),
            pl.BlockSpec((2 * rows, width), lambda s: (s, 0)),
        ] + [fixed(shape) for shape in shapes[6:]],
        compiler_params=pltpu.CompilerParams(vmem_limit_bytes=60 * 1024 * 1024),
        name="finish",
    )(raw_output, raw_grad, units_in, units_in, pairs_in, small)


def split_layer(
    hidden, starts, first_gain, first_shift, qkv_weight, out_weight, second_gain, second_shift,
    up_weight, hidden_bias, down_weight, cotangent,
):
    shards = lax.axis_size("rows")
    (
        qkv_all, out_all, up_all, down_all, dy_all, normed_t, packed, lse, att_t, residual, second_t,
        activated, activated_t, slope,
    ) = forward(
        hidden[0], cotangent[0], starts, first_gain, first_shift, second_gain, second_shift, hidden_bias,
        qkv_weight, out_weight, up_weight, down_weight,
    )
    whole = lambda w: w.reshape(-1, w.shape[-1])
    blocks = lambda w: w.reshape(shards, -1, w.shape[-1])
    shares = backward(
        starts, first_gain, second_gain, hidden[0], dy_all, whole(qkv_all), whole(out_all),
        whole(up_all), whole(down_all), normed_t, packed, lse, blocks(att_t), residual,
        blocks(second_t), activated, blocks(activated_t), slope,
    )
    return tuple(finish(*shares))


def splits_evenly(mesh):
    pieces = mesh.shape["blk"]
    return pieces == 2 and mesh.shape["rows"] == 2 * ROWS_Z * ROWS_Y and HEADS % (2 * pieces) == 0


def solution(mesh):
    in_specs = (
        P("rows", "blk", None),
        P("rows", None),
        P(),
        P(),
        P("rows", None),
        P("rows", None),
        P(),
        P(),
        P("rows", None),
        P(),
        P("rows", None),
        P("rows", "blk", None),
    )
    out_specs = (
        P("rows", "blk", None),
        P("rows", "blk", None),
        P("rows", None),
        P("rows", None),
        P("rows", None),
        P("rows", None),
        P(),
        P(),
        P(),
        P(),
        P(),
    )
    layer = split_layer if splits_evenly(mesh) else on_device
    return jax.shard_map(
        layer, mesh=mesh, in_specs=in_specs, out_specs=out_specs, check_vma=False
    )
```

profile of v0, /device:TPU:0, one launch (start us, length us, event | category | flops | bytes accessed | tf_op | source)
XLA Modules:
  0.0 337.1 jit_solution(13387699139179762776)
XLA Ops:
  0.6 167.1 %forward.1 = (bf16[16,80,1920]{2,1,0:T(8,128)(2,1)}, bf16[16,80,1280]{2,1,0:T(8,128)(2,1)}, bf16[16,80,2560]{2,1,0:T(8,128)(2,1)}, bf16[16,160,1280]{2,1,0:T(8,1...) custom-call(bf16[384,1280]{1,0:T(8,128)(2,1)} %bitcast.13, ...), custom_call_target="tpu_custom_call" | custom-call | tf_op jit(solution)/shard_map/forward/pallas_call | solution.py:685
  167.7 162.7 %backward.1 = (f32[384,1280]{1,0:T(8,128)}, f32[384,1280]{1,0:T(8,128)}, bf16[2,10,80,640]{3,2,1,0:T(8,128)(2,1)}, bf16[2,5,80,384]{3,2,1,0:T(8,128)(2,1)}, f32[2,8,1280]{2,1,0:T(8,128)}) custom-call(s32[1,4]{1,0:T(1,128)} %starts.3, f32[1280]{0:T(1024)} %gain1.3, f32[1280]{0:T(1024)} %gain2.3, bf16[384,1280]{1,0:T(8,128)(2,1)} %bitcast.14, ...), custom_call_target="tpu_custom_call" | custom-call | tf_op jit(solution)/shard_map/backward/pallas_call | solution.py:1196
  330.4 6.5 %finish.1 = (f32[1,384,1280]{2,1,0:T(8,128)}, f32[1,384,1280]{2,1,0:T(8,128)}, f32[80,3840]{1,0:T(8,128)}, f32[80,1280]{1,0:T(8,128)}, f32[80,5120]{1,0:T(8,128)...) custom-call(f32[384,1280]{1,0:T(8,128)} %get-tuple-element.44.raw_ou, ...), custom_call_target="tpu_custom_call" | custom-call | tf_op jit(solution)/shard_map/finish/pallas_call | solution.py:1275
where the time goes:
time: 337 us
  Pallas kernels  336 us (100%)
    pallas_call x1, Pallas kernels, forward(): pl.pallas_call(forward_kernel, out_shape=[jax.ShapeDtypeStruct(shape, kin...  167 us
    pallas_call x1, Pallas kernels, backward(): pl.pallas_call(backward_kernel, out_shape=[jax.ShapeDtypeStruct(shape, ki...  163 us

commit v1 on v0

--- a/solution.py
+++ b/solution.py
@@ -323,11 +323,11 @@
 
 
 def forward_kernel(
-    hidden, cot, starts, gain1, shift1, gain2, shift2, bias_in, q_in, o_own, u_in, d_in,
+    hidden, cot, starts, gain1, shift1, gain2, shift2, bias_in, q_in, o_in, u_in, d_in,
     q_all, o_all, u_all, d_all, dy_all, normed_t_out, packed_out, lse_out, att_t_out, resid_out,
     second_t_out, act_out, act_t_out, slope_out,
     hid_other, normed, wq, wo, wu, packed, mask, att_part, att_own, resid, second,
-    act, act_t, slope, normed_t, att_t, second_t, lse, u_wide, u_own, bias,
+    act, act_t, slope, normed_t, att_t, second_t, lse, u_wide, q_own, o_own, u_own, d_own, cot_own, bias,
     local_sem, send_sem, recv_sem, x_send, x_recv,
 ):
     bf16 = jnp.bfloat16
@@ -337,9 +337,16 @@
     other = 1 - piece
     own_rows, width = hidden.shape
     length = packed.shape[0]
-    d_own = d_in.at[pl.ds(piece * d_all.shape[1], d_all.shape[1])]
-    own = (q_all.at[me], o_own, u_own, d_own)
-    gathered = (q_all, o_all, u_all, d_all)
+    rows = o_own.shape[0]
+    d_rows = lambda ref, half: ref.at[pl.ds(half * rows, rows)]
+    own = (q_own, o_own, u_own, d_rows(d_own, 0), d_rows(d_own, 1))
+
+    def slot_of(w, at_z, at_y, at_core):
+        slot = row_of(at_z, at_y, at_core)
+        if w < 3:
+            return (q_all, o_all, u_all)[w].at[slot]
+        return d_rows(d_all.at[slot], w - 3)
+
     x_peer = {"blk": other}
     peers = neighbours()
     pairs = packed.shape[1] // (3 * PAIR)
@@ -350,29 +357,98 @@
     def local(src, dst, index):
         return pltpu.make_async_copy(src, dst, local_sem.at[index])
 
-    def block(w, stage):
-        if stage < 3:
-            slot, peer = me, peers[stage]
-        elif stage < 7:
-            slot, peer = row_of(z - (stage - 3), y, core), peers[3]
-        elif stage < 11:
-            slot, peer = row_of(z - (stage - 7), y, core), peers[4]
-        else:
-            slot, peer = row_of(z - (stage - 11), 1 - y, core), peers[4]
-        src = own[w] if stage in (0, 1, 2, 3, 7) else gathered[w].at[slot]
-        index = w * 15 + stage
+    peer_up, peer_down, peer_y, peer_core = peers[0], peers[2], peers[3], peers[4]
+
+    def send(w, at_z, v, place, peer, first=False):
+        block = slot_of(w, at_z, y if v == 0 else 1 - y, core)
+        index = w * 24 + place
         return pltpu.make_async_remote_copy(
-            src_ref=src, dst_ref=gathered[w].at[slot], send_sem=send_sem.at[index],
+            src_ref=own[w] if first else block, dst_ref=block, send_sem=send_sem.at[index],
             recv_sem=recv_sem.at[index], device_id=peer, device_id_type=MESH,
         )
 
-    def start(w, *stages):
-        for stage in stages:
-            block(w, stage).start()
-
-    def arrived(w, *stages):
-        for stage in stages:
-            block(w, stage).wait_recv()
+    def along(w, side, a, v):
+        at_z = z - (a - 1) if side == 0 else z + (a - 1)
+        return send(w, at_z, v, (side * 3 + a - 1) * 2 + v, peer_up if side == 0 else peer_down, a == 1 and v == 0)
+
+    def to_y(w, at_z, first=False):
+        return send(w, at_z, 0, 12 + at_z, peer_y, first)
+
+    def to_core(w, at_z, v, first=False):
+        return send(w, at_z, v, 16 + 2 * at_z + v, peer_core, first)
+
+    def pass_on(w, a, v):
+        @pl.when(z < ROWS_Z - 1)
+        def _():
+            along(w, 0, a, v).start()
+
+        @pl.when(z > 0)
+        def _():
+            along(w, 1, a, v).start()
+
+    def from_z(a, action):
+        @pl.when(z >= a)
+        def _():
+            action(0, z - a)
+
+        @pl.when(z + a < ROWS_Z)
+        def _():
+            action(1, z + a)
+
+    def start_own(w):
+        pass_on(w, 1, 0)
+        to_y(w, z, True).start()
+        to_core(w, z, 0, True).start()
+
+    def relay_z(w, a, v=0):
+        def action(side, at_z):
+            along(w, side, a, v).wait_recv()
+            if a < ROWS_Z - 1:
+                @pl.when(z < ROWS_Z - 1 if side == 0 else z > 0)
+                def _():
+                    along(w, side, a + 1, v).start()
+
+            if w < 4:
+                to_y(w, at_z).start()
+            to_core(w, at_z, v).start()
+
+        from_z(a, action)
+
+    def relay_y(w, a):
+        def action(side, at_z):
+            to_y(w, at_z).wait_recv()
+            to_core(w, at_z, 1).start()
+
+        if a == 0:
+            action(0, z)
+            if w == 4:
+                pass_on(w, 1, 1)
+        else:
+            from_z(a, action)
+
+    def all_here(w):
+        for at_z in range(ROWS_Z):
+            for v in range(2):
+                to_core(w, at_z, v).wait_recv()
+
+    def all_gone(w):
+        for v in range(1 if w < 4 else 2):
+            for a in range(1, ROWS_Z):
+                @pl.when((z < ROWS_Z - 1) & (z >= a - 1))
+                def _():
+                    along(w, 0, a, v).wait_send()
+
+                @pl.when((z > 0) & (z + a - 1 < ROWS_Z))
+                def _():
+                    along(w, 1, a, v).wait_send()
+
+        for at_z in range(ROWS_Z):
+            if w < 4:
+                to_y(w, at_z).wait_send()
+            for v in range(2):
+                to_core(w, at_z, v).wait_send()
+        if w == 4:
+            to_y(w, z).wait_send()
 
     def to_x(src, dst, index):
         return pltpu.make_async_remote_copy(
@@ -380,36 +456,33 @@
             device_id=x_peer, device_id_type=MESH,
         )
 
-    def relay_z(w, k):
-        arrived(w, k - 1)
-        start(w, 3 + k, 7 + k)
-
-    def relay_y(w, k):
-        arrived(w, 3 + k)
-        start(w, 11 + k)
-
     third = q_in.shape[1] // 3
     share = third // 2
     q_picks = []
     for part in range(3):
         picked = q_in.at[:, pl.ds(pl.multiple_of(part * third + piece * share, 128), share)]
-        q_picks.append(local(picked, q_all.at[me, :, pl.ds(part * share, share)], 17 + part))
+        q_picks.append(local(picked, q_own.at[:, pl.ds(part * share, share)], 17 + part))
         q_picks[-1].start()
+    d_mine = d_in.at[pl.ds(piece * 2 * rows, 2 * rows)]
+    local(o_in, o_own, 1).start()
     local(u_in, u_wide, 2).start()
+    local(d_mine, d_own, 3).start()
+    local(cot, cot_own, 4).start()
     greet(peers)
     for copy in q_picks:
         copy.wait()
-    start(0, 0, 2, 1)
-    start(0, 3, 7)
-    start(1, 0, 2, 1)
-    start(1, 7)
+    start_own(0)
     hidden_x = to_x(hidden, hid_other, 0)
     hidden_x.start()
     cot_x = to_x(cot, dy_all.at[piece], 1)
     cot_x.start()
+    local(q_own, q_all.at[me], 0).start()
+    local(o_in, o_own, 1).wait()
     local(o_own, o_all.at[me], 1).start()
+    local(d_mine, d_own, 3).wait()
     local(d_own, d_all.at[me], 3).start()
-    local(cot, dy_all.at[piece], 4).start()
+    local(cot, cot_own, 4).wait()
+    local(cot_own, dy_all.at[piece], 4).start()
 
     def norm_rows(read, half):
         step = 64
@@ -422,7 +495,7 @@
 
         lax.fori_loop(0, own_rows // step, body, 0)
 
-    units_each = d_all.shape[1]
+    units_each = 2 * rows
     group = 8 * units_each
 
     def mine(block):
@@ -438,22 +511,20 @@
         cols = slice(g * group // 2, (g + 1) * group // 2)
         u_own[:, cols] = mine(u_wide[:, g * group : (g + 1) * group]).astype(bf16)
         bias[:, cols] = mine(bias_in[g * group : (g + 1) * group].reshape(1, group))
-    start(2, 0, 2, 1)
-    start(2, 7)
-    start(3, 0, 2, 1)
-    start(3, 7)
     local(u_own, u_all.at[me], 2).start()
     norm_rows(lambda rows: hidden[rows, :], piece)
     relay_z(0, 1)
+    start_own(1)
+    relay_y(0, 0)
+    write_mask(starts, mask)
+    relay_z(0, 2)
+    relay_y(0, 1)
     relay_z(0, 3)
-    start(1, 3)
-    write_mask(starts, mask)
-    relay_y(0, 0)
-    relay_y(0, 1)
+    relay_y(0, 2)
     hidden_x.wait_recv()
     norm_rows(lambda rows: hid_other[rows, :], other)
-    relay_z(0, 2)
-    relay_y(0, 3)
+    relay_z(1, 1)
+    start_own(2)
 
     def flip(i, carry):
         normed_t[aligned(i, 128), :] = normed[:, aligned(i, 128)].T
@@ -461,11 +532,10 @@
 
     lax.fori_loop(0, width // 128, flip, 0)
     local(normed_t, normed_t_out, 8).start()
-    relay_z(1, 1)
-    relay_y(0, 2)
-    relay_z(1, 3)
-    start(2, 3)
-    arrived(0, *range(7, 15))
+    relay_y(0, 3)
+    relay_z(1, 2)
+    all_here(0)
+    local(q_own, q_all.at[me], 0).wait()
     local(q_all, wq, 5).start()
     local(q_all, wq, 5).wait()
 
@@ -479,7 +549,10 @@
         packed[:, cols] = value * factor
         return carry
 
+    relay_z(1, 3)
+    relay_y(1, 0)
     lax.fori_loop(0, pairs, project, 0)
+    relay_y(1, 1)
     local(packed, packed_out, 9).start()
     first_lanes = head_lanes(PAIR)
 
@@ -519,21 +592,23 @@
         mine = att_part[pl.ds(pl.multiple_of(piece * own_rows, 128), own_rows), p * PAIR : (p + 1) * PAIR]
         att_own[:, att_cols(piece, p)] = mine
         if p == 0:
-            relay_y(1, 0)
-            relay_y(1, 1)
+            relay_y(1, 2)
+            start_own(3)
         elif p == 1:
-            relay_z(1, 2)
+            relay_z(2, 1)
+            start_own(4)
+            relay_y(1, 3)
         elif p == 2:
-            relay_y(1, 3)
+            relay_y(2, 0)
         elif p == 3:
-            relay_z(2, 1)
+            relay_z(2, 2)
         elif p == 4:
-            relay_y(1, 2)
+            relay_y(4, 0)
     local(lse, lse_out, 10).start()
     for copy in att_x:
         copy.wait_recv()
-    arrived(1, *range(7, 15))
-    local(own[1], gathered[1].at[me], 1).wait()
+    all_here(1)
+    local(o_own, o_all.at[me], 1).wait()
     local(o_all, wo, 6).start()
 
     def flip_att(i, carry):
@@ -542,8 +617,7 @@
 
     lax.fori_loop(0, width // 128, flip_att, 0)
     local(att_t, att_t_out, 11).start()
-    relay_z(2, 3)
-    start(3, 3)
+    relay_y(2, 1)
     local(o_all, wo, 6).wait()
 
     def merge(i, carry):
@@ -563,9 +637,13 @@
     lax.fori_loop(0, own_rows // 64, second_rows, 0)
     second_x = to_x(second.at[piece], second.at[piece], 2 + pairs)
     second_x.start()
-    relay_y(2, 0)
-    relay_y(2, 1)
-    relay_z(2, 2)
+    relay_z(2, 3)
+    relay_y(2, 2)
+    relay_z(3, 1)
+    relay_z(3, 2)
+    relay_y(2, 3)
+    relay_y(3, 0)
+    relay_z(3, 3)
     second_x.wait_recv()
 
     def flip_second(i, carry):
@@ -575,14 +653,13 @@
 
     lax.fori_loop(0, width // 128, flip_second, 0)
     local(second_t, second_t_out, 13).start()
-    relay_y(2, 3)
-    relay_z(3, 1)
-    relay_y(2, 2)
-    arrived(2, *range(7, 15))
-    local(own[2], gathered[2].at[me], 2).wait()
+    relay_z(4, 1, 0)
+    relay_y(3, 1)
+    all_here(2)
+    local(u_own, u_all.at[me], 2).wait()
     local(u_all, wu, 7).start()
+    relay_z(4, 1, 1)
     local(u_all, wu, 7).wait()
-    relay_z(3, 3)
     unit = 256
     steps = act.shape[1] // unit
 
@@ -599,20 +676,24 @@
         slope[rows, cols] = (cdf + up * pdf).astype(bf16)
         return carry
 
-    lax.fori_loop(0, steps, expand, 0)
-    relay_y(3, 0)
-    relay_y(3, 1)
-    lax.fori_loop(steps, 2 * steps, expand, 0)
+    lax.fori_loop(0, steps // 2, expand, 0)
+    relay_z(4, 2, 0)
+    relay_y(3, 2)
+    lax.fori_loop(steps // 2, steps, expand, 0)
+    relay_z(4, 2, 1)
+    lax.fori_loop(steps, 3 * steps // 2, expand, 0)
+    relay_z(4, 3, 0)
+    relay_y(3, 3)
+    lax.fori_loop(3 * steps // 2, 2 * steps, expand, 0)
     local(act, act_out, 14).start()
     local(act_t, act_t_out, 15).start()
     local(slope, slope_out, 16).start()
-    relay_z(3, 2)
-    relay_y(3, 3)
-    relay_y(3, 2)
-    arrived(3, *range(7, 15))
+    relay_z(4, 3, 1)
+    all_here(3)
+    all_here(4)
     cot_x.wait_recv()
-    local(own[3], gathered[3].at[me], 3).wait()
-    local(cot, dy_all.at[piece], 4).wait()
+    local(d_own, d_all.at[me], 3).wait()
+    local(cot_own, dy_all.at[piece], 4).wait()
     local(normed_t, normed_t_out, 8).wait()
     local(packed, packed_out, 9).wait()
     local(lse, lse_out, 10).wait()
@@ -622,9 +703,8 @@
     local(act, act_out, 14).wait()
     local(act_t, act_t_out, 15).wait()
     local(slope, slope_out, 16).wait()
-    for w in range(4):
-        for stage in range(15):
-            block(w, stage).wait_send()
+    for w in range(5):
+        all_gone(w)
     for copy in [hidden_x, cot_x, second_x] + att_x:
         copy.wait_send()
 
@@ -674,7 +754,11 @@
         ((width, length), bf16),
         ((head_rows, length), f32),
         ((rows, 2 * units), bf16),
+        ((rows, cols), bf16),
+        ((rows, width), bf16),
         ((rows, units), bf16),
+        ((2 * rows, width), bf16),
+        ((own_rows, width), bf16),
         ((1, units), f32),
     ]
     vmem = pl.BlockSpec(memory_space=pltpu.VMEM)
@@ -688,7 +772,7 @@
         in_specs=[vmem, anywhere, smem] + [vmem] * 5 + [anywhere] * 4,
         out_specs=[anywhere] * len(outs),
         scratch_shapes=[pltpu.VMEM(shape, kind) for shape, kind in scratch]
-        + [dma((20,)), dma((60,)), dma((60,)), dma((x_copies,)), dma((x_copies,))],
+        + [dma((20,)), dma((120,)), dma((120,)), dma((x_copies,)), dma((x_copies,))],
         compiler_params=pltpu.CompilerParams(
             collective_id=1, has_side_effects=True, vmem_limit_bytes=60 * 1024 * 1024
         ),

time: 337 us -> 309 us (0.917)
  Pallas kernels: 336 us -> 308 us
    pallas_call x1, Pallas kernels: 167 us -> 144 us  [forward(): pl.pallas_call(forward_kernel, out_shape=[jax.ShapeDtypeStruct(shape, kin...]
    pallas_call x1, Pallas kernels: 163 us -> 158 us  [backward(): pl.pallas_call(backward_kernel, out_shape=[jax.ShapeDtypeStruct(shape, ki...]
where the time goes in v1:
time: 309 us
  Pallas kernels  308 us (100%)
    pallas_call x1, Pallas kernels, backward(): pl.pallas_call(backward_kernel, out_shape=[jax.ShapeDtypeStruct(shape, ki...  158 us
    pallas_call x1, Pallas kernels, forward(): pl.pallas_call(forward_kernel, out_shape=[jax.ShapeDtypeStruct(shape, kin...  144 us
    pallas_call x1, Pallas kernels, finish(): pl.pallas_call(finish_kernel, grid=(2,), out_shape=[jax.ShapeDtypeStruct(...  6.48 us

profile of v1, /device:TPU:0, one launch (start us, length us, event | category | flops | bytes accessed | tf_op | source)
XLA Modules:
  0.0 308.5 jit_solution(15787252673083589198)
XLA Ops:
  0.6 143.5 %forward.1 = (bf16[16,80,1920]{2,1,0:T(8,128)(2,1)}, bf16[16,80,1280]{2,1,0:T(8,128)(2,1)}, bf16[16,80,2560]{2,1,0:T(8,128)(2,1)}, bf16[16,160,1280]{2,1,0:T(8,1...) custom-call(bf16[384,1280]{1,0:T(8,128)(2,1)} %bitcast.13, ...), custom_call_target="tpu_custom_call" | custom-call | tf_op jit(solution)/shard_map/forward/pallas_call | solution.py:769
  144.2 157.7 %backward.1 = (f32[384,1280]{1,0:T(8,128)}, f32[384,1280]{1,0:T(8,128)}, bf16[2,10,80,640]{3,2,1,0:T(8,128)(2,1)}, bf16[2,5,80,384]{3,2,1,0:T(8,128)(2,1)}, f32[2,8,1280]{2,1,0:T(8,128)}) custom-call(s32[1,4]{1,0:T(1,128)} %starts.3, f32[1280]{0:T(1024)} %gain1.3, f32[1280]{0:T(1024)} %gain2.3, bf16[384,1280]{1,0:T(8,128)(2,1)} %bitcast.14, ...), custom_call_target="tpu_custom_call" | custom-call | tf_op jit(solution)/shard_map/backward/pallas_call | solution.py:1280
  301.8 6.5 %finish.1 = (f32[1,384,1280]{2,1,0:T(8,128)}, f32[1,384,1280]{2,1,0:T(8,128)}, f32[80,3840]{1,0:T(8,128)}, f32[80,1280]{1,0:T(8,128)}, f32[80,5120]{1,0:T(8,128)...) custom-call(f32[384,1280]{1,0:T(8,128)} %get-tuple-element.44.raw_ou, ...), custom_call_target="tpu_custom_call" | custom-call | tf_op jit(solution)/shard_map/finish/pallas_call | solution.py:1359

commit v2 on v0

--- a/solution.py
+++ b/solution.py
@@ -1,3 +1,4 @@
+import functools
 import math
 
 import jax
@@ -255,6 +256,64 @@
 
 
 MESH = pl.DeviceIdType.MESH
+FORWARD_MOVES = (
+    ((0, 0), (1, 0), (2, 0), (0, 1), (1, 1), (2, 1),),
+    (),
+    (),
+    (),
+    (),
+    (),
+    (),
+    (),
+    (),
+    (),
+    ((3, 0, 1, 0), (4, 0, 0), (4, 1, 0), (3, 0, 0, 0), (0, 2), (3, 1, 1, 0), (4, 0, 2), (3, 1, 0, 0), (4, 0, 1), (3, 0, 2, 0), (4, 1, 2), (4, 1, 1), (3, 2, 1, 0), (2, 4),),
+    (),
+    (),
+    ((4, 0, 3), (3, 2, 0, 0), (0, 3), (4, 2, 2), (3, 1, 2, 0), (1, 2), (4, 2, 1), (3, 2, 2, 0), (1, 3), (4, 1, 3),),
+    (),
+    (),
+    ((4, 2, 0), (3, 3, 1, 0), (0, 5), (2, 5),),
+    ((4, 2, 3),),
+    (),
+    (),
+    (),
+    (),
+    (),
+    ((3, 3, 0, 0),),
+    (),
+    (),
+    ((4, 3, 0), (2, 2), (2, 3), (0, 4),),
+    (),
+    ((3, 5, 1, 0),),
+    (),
+    (),
+    (),
+    ((3, 5, 0, 0),),
+    (),
+    (),
+    ((4, 3, 2),),
+    (),
+    (),
+    (),
+    (),
+    ((3, 3, 2, 0), (1, 5), (4, 3, 1), (1, 4), (3, 4, 1, 0), (3, 4, 0, 0), (4, 3, 3), (3, 5, 2, 0),),
+    (),
+    ((4, 5, 0),),
+    ((3, 4, 2, 0),),
+    (),
+    ((4, 4, 0),),
+    (),
+    ((3, 5, 1, 1),),
+    (),
+    (),
+    ((4, 4, 2),),
+    (),
+    ((3, 5, 0, 1),),
+    (),
+    ((4, 4, 1),),
+    ((3, 5, 2, 1), (4, 4, 3),),
+)
 ROWS_Z, ROWS_Y = 4, 2
 PAIR = 128
 
@@ -304,7 +363,7 @@
     ]
 
 
-def write_mask(starts_ref, mask_ref):
+def write_mask(starts_ref, mask_ref, part=0, parts=1):
     blocks, step, length = mask_ref.shape
 
     def rows(i, carry):
@@ -319,15 +378,15 @@
         mask_ref[i] = jnp.where(key_seg == query_seg, 0.0, masked_score).astype(mask_ref.dtype)
         return carry
 
-    lax.fori_loop(0, blocks, rows, 0)
+    lax.fori_loop(blocks * part // parts, blocks * (part + 1) // parts, rows, 0)
 
 
 def forward_kernel(
-    hidden, cot, starts, gain1, shift1, gain2, shift2, bias_in, q_in, o_own, u_in, d_in,
+    hidden, cot, starts, gain1, shift1, gain2, shift2, bias_in, q_in, o_in, u_in, d_in,
     q_all, o_all, u_all, d_all, dy_all, normed_t_out, packed_out, lse_out, att_t_out, resid_out,
     second_t_out, act_out, act_t_out, slope_out,
     hid_other, normed, wq, wo, wu, packed, mask, att_part, att_own, resid, second,
-    act, act_t, slope, normed_t, att_t, second_t, lse, u_wide, u_own, bias,
+    act, act_t, slope, normed_t, att_t, second_t, lse, u_wide, q_own, o_own, u_own, d_own, cot_own, bias,
     local_sem, send_sem, recv_sem, x_send, x_recv,
 ):
     bf16 = jnp.bfloat16
@@ -337,9 +396,23 @@
     other = 1 - piece
     own_rows, width = hidden.shape
     length = packed.shape[0]
-    d_own = d_in.at[pl.ds(piece * d_all.shape[1], d_all.shape[1])]
-    own = (q_all.at[me], o_own, u_own, d_own)
-    gathered = (q_all, o_all, u_all, d_all)
+    rows = o_own.shape[0]
+    early = rows * 3 // 5
+    d_half = lambda half: pl.ds(half * rows, rows)
+    own = (
+        q_own.at[pl.ds(0, early)], q_own.at[pl.ds(early, rows - early)], o_own, u_own,
+        d_own.at[d_half(0)], d_own.at[d_half(1)],
+    )
+    last = len(own) - 1
+
+    def slot_of(w, at_z, at_y, at_core):
+        slot = row_of(at_z, at_y, at_core)
+        if w < 2:
+            return q_all.at[slot, pl.ds(w * early, own[w].shape[0])]
+        if w < 4:
+            return (o_all, u_all)[w - 2].at[slot]
+        return d_all.at[slot, d_half(w - 4)]
+
     x_peer = {"blk": other}
     peers = neighbours()
     pairs = packed.shape[1] // (3 * PAIR)
@@ -350,29 +423,84 @@
     def local(src, dst, index):
         return pltpu.make_async_copy(src, dst, local_sem.at[index])
 
-    def block(w, stage):
-        if stage < 3:
-            slot, peer = me, peers[stage]
-        elif stage < 7:
-            slot, peer = row_of(z - (stage - 3), y, core), peers[3]
-        elif stage < 11:
-            slot, peer = row_of(z - (stage - 7), y, core), peers[4]
-        else:
-            slot, peer = row_of(z - (stage - 11), 1 - y, core), peers[4]
-        src = own[w] if stage in (0, 1, 2, 3, 7) else gathered[w].at[slot]
-        index = w * 15 + stage
+    near = z + 1 - 2 * lax.rem(z, 2)
+    far = lax.rem(z + 2, ROWS_Z)
+    spread = (z, far, near, ROWS_Z - 1 - z)
+
+    def send(w, at_z, v, place, peer, first=False):
+        block = slot_of(w, at_z, y if v == 0 else 1 - y, core)
+        index = w * 18 + place
         return pltpu.make_async_remote_copy(
-            src_ref=src, dst_ref=gathered[w].at[slot], send_sem=send_sem.at[index],
+            src_ref=own[w] if first else block, dst_ref=block, send_sem=send_sem.at[index],
             recv_sem=recv_sem.at[index], device_id=peer, device_id_type=MESH,
         )
 
-    def start(w, *stages):
-        for stage in stages:
-            block(w, stage).start()
-
-    def arrived(w, *stages):
-        for stage in stages:
-            block(w, stage).wait_recv()
+    def along(w, k, v):
+        peer = {"rows": row_of(far if k == 0 else near, y, core)}
+        return send(w, far if k == 2 else z, v, 2 * k + v, peer, k < 2 and v == 0)
+
+    def to_y(w, at_z, first=False):
+        return send(w, at_z, 0, 6 + at_z, peers[3], first)
+
+    def to_core(w, at_z, v, first=False):
+        return send(w, at_z, v, 10 + 2 * at_z + v, peers[4], first)
+
+    def pass_on(w, v):
+        inner = (z == 1) | (z == 2)
+
+        @pl.when(inner)
+        def _():
+            along(w, 0, v).start()
+
+        along(w, 1, v).start()
+
+        @pl.when(jnp.logical_not(inner))
+        def _():
+            along(w, 0, v).start()
+
+    def relay_z(w, k, v):
+        along(w, k, v).wait_recv()
+        if k == 0:
+            along(w, 2, v).start()
+        at_z = spread[k + 1]
+        if w < last:
+            to_y(w, at_z).start()
+        to_core(w, at_z, v).start()
+
+    def relay_y(w, k):
+        to_y(w, spread[k]).wait_recv()
+        to_core(w, spread[k], 1).start()
+        if w == last:
+            pass_on(w, 1)
+
+    def all_here(ws):
+        for w in ws:
+            for at_z in range(ROWS_Z):
+                for v in range(2):
+                    to_core(w, at_z, v).wait_recv()
+
+    def all_here_load(ws, source, target, first):
+        for i, at_z in enumerate(spread):
+            for v in range(2):
+                for w in ws:
+                    to_core(w, at_z, v).wait_recv()
+                chip = pl.ds(row_of(at_z, y if v == 0 else 1 - y, 0), 2)
+                local(source.at[chip], target.at[chip], first + 2 * i + v).start()
+
+    def loaded(source, target, first):
+        for i in range(2 * ROWS_Z):
+            chip = pl.ds(0, 2)
+            local(source.at[chip], target.at[chip], first + i).wait()
+
+    def all_gone(w):
+        for v in range(1 if w < last else 2):
+            for k in range(3):
+                along(w, k, v).wait_send()
+        for at_z in range(ROWS_Z) if w < last else (z,):
+            to_y(w, at_z).wait_send()
+        for at_z in range(ROWS_Z):
+            for v in range(2):
+                to_core(w, at_z, v).wait_send()
 
     def to_x(src, dst, index):
         return pltpu.make_async_remote_copy(
@@ -380,49 +508,36 @@
             device_id=x_peer, device_id_type=MESH,
         )
 
-    def relay_z(w, k):
-        arrived(w, k - 1)
-        start(w, 3 + k, 7 + k)
-
-    def relay_y(w, k):
-        arrived(w, 3 + k)
-        start(w, 11 + k)
-
     third = q_in.shape[1] // 3
     share = third // 2
     q_picks = []
     for part in range(3):
         picked = q_in.at[:, pl.ds(pl.multiple_of(part * third + piece * share, 128), share)]
-        q_picks.append(local(picked, q_all.at[me, :, pl.ds(part * share, share)], 17 + part))
+        q_picks.append(local(picked, q_own.at[:, pl.ds(part * share, share)], 17 + part))
         q_picks[-1].start()
+    d_mine = d_in.at[pl.ds(piece * 2 * rows, 2 * rows)]
+    local(o_in, o_own, 1).start()
     local(u_in, u_wide, 2).start()
+    local(d_mine, d_own, 3).start()
+    local(cot, cot_own, 4).start()
     greet(peers)
     for copy in q_picks:
         copy.wait()
-    start(0, 0, 2, 1)
-    start(0, 3, 7)
-    start(1, 0, 2, 1)
-    start(1, 7)
     hidden_x = to_x(hidden, hid_other, 0)
-    hidden_x.start()
     cot_x = to_x(cot, dy_all.at[piece], 1)
-    cot_x.start()
-    local(o_own, o_all.at[me], 1).start()
-    local(d_own, d_all.at[me], 3).start()
-    local(cot, dy_all.at[piece], 4).start()
-
-    def norm_rows(read, half):
-        step = 64
-
-        def body(i, carry):
-            rows = read(aligned(i, step)).astype(jnp.float32)
-            low = layer_norm(rows, first_gain, first_shift).astype(bf16)
-            normed[pl.ds(pl.multiple_of(half * own_rows + i * step, step), step), :] = low
-            return carry
-
-        lax.fori_loop(0, own_rows // step, body, 0)
-
-    units_each = d_all.shape[1]
+    local(o_in, o_own, 1).wait()
+    local(d_mine, d_own, 3).wait()
+    local(u_in, u_wide, 2).wait()
+    half_rows = lambda half: pl.ds(pl.multiple_of(half * own_rows, 128), own_rows)
+
+    def first_copies():
+        local(q_own, q_all.at[me], 0).start()
+        local(o_own, o_all.at[me], 1).start()
+        local(d_own, d_all.at[me], 3).start()
+        local(cot, cot_own, 4).wait()
+        local(cot_own, dy_all.at[piece], 4).start()
+
+    units_each = 2 * rows
     group = 8 * units_each
 
     def mine(block):
@@ -433,199 +548,230 @@
             halves.append(jnp.concatenate([wide[:, cols] for cols in at], axis=1))
         return jnp.where(piece == 0, halves[0], halves[1])
 
-    local(u_in, u_wide, 2).wait()
-    for g in range(u_own.shape[1] // (group // 2)):
+    def pick_units(g):
         cols = slice(g * group // 2, (g + 1) * group // 2)
         u_own[:, cols] = mine(u_wide[:, g * group : (g + 1) * group]).astype(bf16)
         bias[:, cols] = mine(bias_in[g * group : (g + 1) * group].reshape(1, group))
-    start(2, 0, 2, 1)
-    start(2, 7)
-    start(3, 0, 2, 1)
-    start(3, 7)
-    local(u_own, u_all.at[me], 2).start()
-    norm_rows(lambda rows: hidden[rows, :], piece)
-    relay_z(0, 1)
-    relay_z(0, 3)
-    start(1, 3)
-    write_mask(starts, mask)
-    relay_y(0, 0)
-    relay_y(0, 1)
-    hidden_x.wait_recv()
-    norm_rows(lambda rows: hid_other[rows, :], other)
-    relay_z(0, 2)
-    relay_y(0, 3)
-
-    def flip(i, carry):
-        normed_t[aligned(i, 128), :] = normed[:, aligned(i, 128)].T
-        return carry
-
-    lax.fori_loop(0, width // 128, flip, 0)
-    local(normed_t, normed_t_out, 8).start()
-    relay_z(1, 1)
-    relay_y(0, 2)
-    relay_z(1, 3)
-    start(2, 3)
-    arrived(0, *range(7, 15))
-    local(q_all, wq, 5).start()
-    local(q_all, wq, 5).wait()
+        if g == u_own.shape[1] * 2 // group - 1:
+            local(u_own, u_all.at[me], 2).start()
+
+    def norm_rows(source, half, part):
+        step = 64
+        steps = own_rows // step
+
+        def body(i, carry):
+            value = source[aligned(i, step), :].astype(jnp.float32)
+            low = layer_norm(value, first_gain, first_shift).astype(bf16)
+            normed[pl.ds(pl.multiple_of(half * own_rows + i * step, step), step), :] = low
+            return carry
+
+        lax.fori_loop(steps * part // 2, steps * (part + 1) // 2, body, 0)
+
+    def q_here():
+        local(q_own, q_all.at[me], 0).wait()
+        all_here_load((0, 1), q_all, wq, 20)
 
     column = lax.broadcasted_iota(jnp.int32, (1, 3 * PAIR), 1)
 
-    def project(i, carry):
-        cols = aligned(i, 3 * PAIR)
-        weight = wq[:, :, cols].reshape(width, 3 * PAIR)
-        value = dot_nn(normed[...], weight).astype(bf16)
-        factor = jnp.where(i * 3 * PAIR + column < share, HEAD_DIM ** (-0.5), 1.0).astype(bf16)
-        packed[:, cols] = value * factor
-        return carry
-
-    lax.fori_loop(0, pairs, project, 0)
-    local(packed, packed_out, 9).start()
+    def project(begin, end):
+        def body(i, carry):
+            cols = aligned(i, 3 * PAIR)
+            weight = wq[:, :, cols].reshape(width, 3 * PAIR)
+            value = dot_nn(normed[...], weight).astype(bf16)
+            factor = jnp.where(i * 3 * PAIR + column < share, HEAD_DIM ** (-0.5), 1.0).astype(bf16)
+            packed[:, cols] = value * factor
+            return carry
+
+        lax.fori_loop(begin, end, body, 0)
+        if end == pairs:
+            local(packed, packed_out, 9).start()
+
     first_lanes = head_lanes(PAIR)
 
-    def attend(p):
+    def att_cols(half, p):
+        return pl.ds(pl.multiple_of(half * pairs * PAIR + p * PAIR, PAIR), PAIR)
+
+    def attend(p, half):
         at_q, at_k, at_v = (slice(t * share + PAIR * p, t * share + PAIR * (p + 1)) for t in range(3))
         value_t = packed[:, at_v].T
-        step = 256
-
-        def rows(i, carry):
-            queries = packed[aligned(i, step), at_q]
-            keys = packed[:, at_k]
-            halves = []
-            for h in range(2):
-                one = jnp.where(first_lanes[h], queries, jnp.zeros_like(queries))
-                scores = dot_nt(keys, one) + mask[:, :, aligned(i, step)].reshape(length, step)
-                top = jnp.max(scores, axis=0, keepdims=True)
-                weights = jnp.exp(scores - top)
-                total = jnp.sum(weights, axis=0, keepdims=True)
-                lse[2 * p + h : 2 * p + h + 1, aligned(i, step)] = top + jnp.log(total)
-                summed = dot_nn(value_t[h * HEAD_DIM : (h + 1) * HEAD_DIM], weights.astype(bf16))
-                halves.append(summed / total)
-            both = jnp.concatenate(halves, axis=0).T.astype(bf16)
-            att_part[aligned(i, step), p * PAIR : (p + 1) * PAIR] = both
+        at = half_rows(half)
+        queries = packed[at, at_q]
+        keys = packed[:, at_k]
+        halves = []
+        for h in range(2):
+            one = jnp.where(first_lanes[h], queries, jnp.zeros_like(queries))
+            scores = dot_nt(keys, one) + mask[:, :, at].reshape(length, own_rows)
+            top = jnp.max(scores, axis=0, keepdims=True)
+            weights = jnp.exp(scores - top)
+            total = jnp.sum(weights, axis=0, keepdims=True)
+            lse[2 * p + h : 2 * p + h + 1, at] = top + jnp.log(total)
+            summed = dot_nn(value_t[h * HEAD_DIM : (h + 1) * HEAD_DIM], weights.astype(bf16))
+            halves.append(summed / total)
+        return jnp.concatenate(halves, axis=0).T.astype(bf16)
+
+    def attend_other(p):
+        att_part[:, p * PAIR : (p + 1) * PAIR] = attend(p, other)
+
+    def attend_own(p):
+        att_own[:, att_cols(piece, p)] = attend(p, piece)
+        if p == pairs - 1:
+            local(lse, lse_out, 10).start()
+
+    att_x = [
+        to_x(att_part.at[:, pl.ds(p * PAIR, PAIR)], att_own.at[:, att_cols(piece, p)], 2 + p) for p in range(pairs)
+    ]
+
+    def o_here():
+        local(o_own, o_all.at[me], 1).wait()
+        all_here_load((2,), o_all, wo, 28)
+
+    def att_here():
+        for copy in att_x:
+            copy.wait_recv()
+        loaded(o_all, wo, 28)
+
+    part_rows = own_rows // 2
+    second_x = [
+        to_x(second.at[piece, pl.ds(i * part_rows, part_rows)], second.at[piece, pl.ds(i * part_rows, part_rows)], 2 + pairs + i)
+        for i in range(2)
+    ]
+
+    def merge(part):
+        at = slice(part * part_rows, (part + 1) * part_rows)
+
+        def body(i, carry):
+            cols = aligned(i, 256)
+            weight = wo[:, :, cols].reshape(width, 256)
+            resid[at, cols] = hidden[at, cols].astype(jnp.float32) + dot_nn(att_own[at, :], weight)
             return carry
 
-        lax.fori_loop(0, length // step, rows, 0)
-
-    def att_cols(half, p):
-        return pl.ds(pl.multiple_of(half * pairs * PAIR + p * PAIR, PAIR), PAIR)
-
-    att_x = []
+        lax.fori_loop(0, width // 256, body, 0)
+
+        def second_rows(i, carry):
+            rows = aligned(i, 64)
+            second[piece, rows, :] = layer_norm(resid[rows, :], second_gain, second_shift).astype(bf16)
+            return carry
+
+        lax.fori_loop(part * part_rows // 64, (part + 1) * part_rows // 64, second_rows, 0)
+        if part == 1:
+            local(resid, resid_out, 12).start()
+
+    def flip_normed():
+        def body(i, carry):
+            normed_t[aligned(i, 128), :] = normed[:, aligned(i, 128)].T
+            return carry
+
+        lax.fori_loop(0, width // 128, body, 0)
+        local(normed_t, normed_t_out, 8).start()
+
+    def flip_second(half):
+        def body(i, carry):
+            second_t[aligned(i, 128), half_rows(half)] = second[half, :, aligned(i, 128)].T
+            return carry
+
+        lax.fori_loop(0, width // 128, body, 0)
+
+    def flip_att():
+        def body(i, carry):
+            att_t[aligned(i, 128), :] = att_own[:, aligned(i, 128)].T
+            return carry
+
+        lax.fori_loop(0, width // 128, body, 0)
+        local(att_t, att_t_out, 11).start()
+        flip_second(piece)
+
+    def u_here():
+        local(u_own, u_all.at[me], 2).wait()
+        all_here_load((3,), u_all, wu, 36)
+
+    unit = 256
+    fifth = act.shape[1] // unit // 5
+
+    def expand(half, begin):
+        at = half_rows(half)
+
+        def body(i, carry):
+            cols = aligned(i, unit)
+            weight = wu[:, :, cols].reshape(width, unit)
+            up = dot_nn(second[half], weight) + bias[:, cols]
+            cdf = 0.5 * (1.0 + lax.erf(up * (0.5 ** 0.5)))
+            pdf = jnp.exp(up * up * -0.5) * ((2.0 * math.pi) ** -0.5)
+            value = (up * cdf).astype(bf16)
+            act[at, cols] = value
+            act_t[cols, at] = value.T
+            slope[at, cols] = (cdf + up * pdf).astype(bf16)
+            return carry
+
+        lax.fori_loop(begin * fifth, (begin + 1) * fifth, body, 0)
+        if begin == 4:
+            for copy in halves_out(half):
+                copy.start()
+
+    def halves_out(half):
+        base = 44 if half is piece else 47
+        at = half_rows(half)
+        return (
+            local(act.at[at], act_out.at[at], base),
+            local(act_t.at[:, at], act_t_out.at[:, at], base + 1),
+            local(slope.at[at], slope_out.at[at], base + 2),
+        )
+
+    def second_here():
+        for copy in second_x:
+            copy.wait_recv()
+
+    def flip_last():
+        flip_second(other)
+        local(second_t, second_t_out, 13).start()
+
+    def outputs():
+        local(cot_own, dy_all.at[piece], 4).wait()
+        local(d_own, d_all.at[me], 3).wait()
+        local(normed_t, normed_t_out, 8).wait()
+        local(packed, packed_out, 9).wait()
+        local(lse, lse_out, 10).wait()
+        local(att_t, att_t_out, 11).wait()
+        local(resid, resid_out, 12).wait()
+        local(second_t, second_t_out, 13).wait()
+        for half in (piece, other):
+            for copy in halves_out(half):
+                copy.wait()
+
+    act_now = functools.partial
+    steps = [hidden_x.start, cot_x.start]
+    steps += [act_now(pick_units, g) for g in range(4)]
+    steps += [act_now(norm_rows, hidden, piece, part) for part in range(2)]
+    steps += [act_now(write_mask, starts, mask, part, 2) for part in range(2)]
+    steps += [hidden_x.wait_recv]
+    steps += [act_now(norm_rows, hid_other, other, part) for part in range(2)]
+    steps += [q_here, act_now(loaded, q_all, wq, 20), act_now(project, 0, 2), act_now(project, 2, pairs)]
     for p in range(pairs):
-        attend(p)
-        part = att_part.at[pl.ds(pl.multiple_of(other * own_rows, 128), own_rows), pl.ds(p * PAIR, PAIR)]
-        att_x.append(to_x(part, att_own.at[:, att_cols(piece, p)], 2 + p))
-        att_x[-1].start()
-        mine = att_part[pl.ds(pl.multiple_of(piece * own_rows, 128), own_rows), p * PAIR : (p + 1) * PAIR]
-        att_own[:, att_cols(piece, p)] = mine
-        if p == 0:
-            relay_y(1, 0)
-            relay_y(1, 1)
-        elif p == 1:
-            relay_z(1, 2)
-        elif p == 2:
-            relay_y(1, 3)
-        elif p == 3:
-            relay_z(2, 1)
-        elif p == 4:
-            relay_y(1, 2)
-    local(lse, lse_out, 10).start()
-    for copy in att_x:
-        copy.wait_recv()
-    arrived(1, *range(7, 15))
-    local(own[1], gathered[1].at[me], 1).wait()
-    local(o_all, wo, 6).start()
-
-    def flip_att(i, carry):
-        att_t[aligned(i, 128), :] = att_own[:, aligned(i, 128)].T
-        return carry
-
-    lax.fori_loop(0, width // 128, flip_att, 0)
-    local(att_t, att_t_out, 11).start()
-    relay_z(2, 3)
-    start(3, 3)
-    local(o_all, wo, 6).wait()
-
-    def merge(i, carry):
-        cols = aligned(i, 256)
-        weight = wo[:, :, cols].reshape(width, 256)
-        resid[:, cols] = hidden[:, cols].astype(jnp.float32) + dot_nn(att_own[...], weight)
-        return carry
-
-    lax.fori_loop(0, width // 256, merge, 0)
-    local(resid, resid_out, 12).start()
-
-    def second_rows(i, carry):
-        rows = aligned(i, 64)
-        second[piece, rows, :] = layer_norm(resid[rows, :], second_gain, second_shift).astype(bf16)
-        return carry
-
-    lax.fori_loop(0, own_rows // 64, second_rows, 0)
-    second_x = to_x(second.at[piece], second.at[piece], 2 + pairs)
-    second_x.start()
-    relay_y(2, 0)
-    relay_y(2, 1)
-    relay_z(2, 2)
-    second_x.wait_recv()
-
-    def flip_second(i, carry):
-        cols = aligned(i, 128)
-        second_t[cols, :] = second[:, :, cols].reshape(length, 128).T
-        return carry
-
-    lax.fori_loop(0, width // 128, flip_second, 0)
-    local(second_t, second_t_out, 13).start()
-    relay_y(2, 3)
-    relay_z(3, 1)
-    relay_y(2, 2)
-    arrived(2, *range(7, 15))
-    local(own[2], gathered[2].at[me], 2).wait()
-    local(u_all, wu, 7).start()
-    local(u_all, wu, 7).wait()
-    relay_z(3, 3)
-    unit = 256
-    steps = act.shape[1] // unit
-
-    def expand(i, carry):
-        cols = aligned(i // 2, unit)
-        rows = aligned(lax.rem(i, 2), own_rows)
-        weight = wu[:, :, cols].reshape(width, unit)
-        up = dot_nn(second[lax.rem(i, 2)], weight) + bias[:, cols]
-        cdf = 0.5 * (1.0 + lax.erf(up * (0.5 ** 0.5)))
-        pdf = jnp.exp(up * up * -0.5) * ((2.0 * math.pi) ** -0.5)
-        value = (up * cdf).astype(bf16)
-        act[rows, cols] = value
-        act_t[cols, rows] = value.T
-        slope[rows, cols] = (cdf + up * pdf).astype(bf16)
-        return carry
-
-    lax.fori_loop(0, steps, expand, 0)
-    relay_y(3, 0)
-    relay_y(3, 1)
-    lax.fori_loop(steps, 2 * steps, expand, 0)
-    local(act, act_out, 14).start()
-    local(act_t, act_t_out, 15).start()
-    local(slope, slope_out, 16).start()
-    relay_z(3, 2)
-    relay_y(3, 3)
-    relay_y(3, 2)
-    arrived(3, *range(7, 15))
+        steps += [act_now(attend_other, p), att_x[p].start]
+    steps += [act_now(attend_own, p) for p in range(pairs - 1)]
+    steps += [o_here, act_now(attend_own, pairs - 1), att_here]
+    steps += [act_now(merge, 0), second_x[0].start, act_now(merge, 1), second_x[1].start]
+    steps += [flip_normed, flip_att, u_here, act_now(loaded, u_all, wu, 36)]
+    steps += [act_now(expand, piece, i) for i in range(5)]
+    steps += [second_here, flip_last]
+    steps += [act_now(expand, other, i) for i in range(5)]
+    steps += [outputs, act_now(all_here, (4, 5))]
+    moves = (
+        lambda w: pass_on(w, 0),
+        lambda w: to_y(w, z, True).start(),
+        lambda w: to_core(w, z, 0, True).start(),
+        relay_z,
+        relay_y,
+    )
+    for i, step in enumerate(steps):
+        for kind, *where in FORWARD_MOVES[i]:
+            moves[kind](*where)
+        step()
+        if i == 1:
+            first_copies()
     cot_x.wait_recv()
-    local(own[3], gathered[3].at[me], 3).wait()
-    local(cot, dy_all.at[piece], 4).wait()
-    local(normed_t, normed_t_out, 8).wait()
-    local(packed, packed_out, 9).wait()
-    local(lse, lse_out, 10).wait()
-    local(att_t, att_t_out, 11).wait()
-    local(resid, resid_out, 12).wait()
-    local(second_t, second_t_out, 13).wait()
-    local(act, act_out, 14).wait()
-    local(act_t, act_t_out, 15).wait()
-    local(slope, slope_out, 16).wait()
-    for w in range(4):
-        for stage in range(15):
-            block(w, stage).wait_send()
-    for copy in [hidden_x, cot_x, second_x] + att_x:
+    for w in range(len(own)):
+        all_gone(w)
+    for copy in [hidden_x, cot_x] + second_x + att_x:
         copy.wait_send()
 
 
@@ -662,7 +808,7 @@
         ((shards, rows, units), bf16),
         ((length, cols), bf16),
         ((length // 48, 48, length), f32),
-        ((length, cols // 3), bf16),
+        ((own_rows, cols // 3), bf16),
         ((own_rows, width), bf16),
         ((own_rows, width), f32),
         ((2, own_rows, width), bf16),
@@ -674,21 +820,25 @@
         ((width, length), bf16),
         ((head_rows, length), f32),
         ((rows, 2 * units), bf16),
+        ((rows, cols), bf16),
+        ((rows, width), bf16),
         ((rows, units), bf16),
+        ((2 * rows, width), bf16),
+        ((own_rows, width), bf16),
         ((1, units), f32),
     ]
     vmem = pl.BlockSpec(memory_space=pltpu.VMEM)
     anywhere = pl.BlockSpec(memory_space=pl.ANY)
     smem = pl.BlockSpec(memory_space=pltpu.SMEM)
     dma = pltpu.SemaphoreType.DMA
-    x_copies = 3 + cols // (3 * PAIR)
+    x_copies = 4 + cols // (3 * PAIR)
     return pl.pallas_call(
         forward_kernel,
         out_shape=[jax.ShapeDtypeStruct(shape, kind) for shape, kind in outs],
         in_specs=[vmem, anywhere, smem] + [vmem] * 5 + [anywhere] * 4,
         out_specs=[anywhere] * len(outs),
         scratch_shapes=[pltpu.VMEM(shape, kind) for shape, kind in scratch]
-        + [dma((20,)), dma((60,)), dma((60,)), dma((x_copies,)), dma((x_copies,))],
+        + [dma((50,)), dma((108,)), dma((108,)), dma((x_copies,)), dma((x_copies,))],
         compiler_params=pltpu.CompilerParams(
             collective_id=1, has_side_effects=True, vmem_limit_bytes=60 * 1024 * 1024
         ),

time: 337 us -> 292 us (0.87); the launches traced: 337 us -> 288 us
  Pallas kernels: 336 us -> 287 us
    pallas_call x1, Pallas kernels: 167 us -> 121 us  [forward(): pl.pallas_call(forward_kernel, out_shape=[jax.ShapeDtypeStruct(shape, kin...]
where the time goes in v2:
time: 292 us; the launch traced here: 288 us
  Pallas kernels  287 us (98%)
    pallas_call x1, Pallas kernels, backward(): pl.pallas_call(backward_kernel, out_shape=[jax.ShapeDtypeStruct(shape, ki...  160 us
    pallas_call x1, Pallas kernels, forward(): pl.pallas_call(forward_kernel, out_shape=[jax.ShapeDtypeStruct(shape, kin...  121 us
    pallas_call x1, Pallas kernels, finish(): pl.pallas_call(finish_kernel, grid=(2,), out_shape=[jax.ShapeDtypeStruct(...  6.48 us

profile of v2, /device:TPU:0, one launch (start us, length us, event | category | flops | bytes accessed | tf_op | source)
XLA Modules:
  0.0 288.3 jit_solution(7223953757716190868)
XLA Ops:
  0.6 120.7 %forward.1 = (bf16[16,80,1920]{2,1,0:T(8,128)(2,1)}, bf16[16,80,1280]{2,1,0:T(8,128)(2,1)}, bf16[16,80,2560]{2,1,0:T(8,128)(2,1)}, bf16[16,160,1280]{2,1,0:T(8,1...) custom-call(bf16[384,1280]{1,0:T(8,128)(2,1)} %bitcast.13, ...), custom_call_target="tpu_custom_call" | custom-call | tf_op jit(solution)/shard_map/forward/pallas_call | solution.py:835
  121.4 160.2 %backward.1 = (f32[384,1280]{1,0:T(8,128)}, f32[384,1280]{1,0:T(8,128)}, bf16[2,10,80,640]{3,2,1,0:T(8,128)(2,1)}, bf16[2,5,80,384]{3,2,1,0:T(8,128)(2,1)}, f32[2,8,1280]{2,1,0:T(8,128)}) custom-call(s32[1,4]{1,0:T(1,128)} %starts.3, f32[1280]{0:T(1024)} %gain1.3, f32[1280]{0:T(1024)} %gain2.3, bf16[384,1280]{1,0:T(8,128)(2,1)} %bitcast.14, ...), custom_call_target="tpu_custom_call" | custom-call | tf_op jit(solution)/shard_map/backward/pallas_call | solution.py:1346
  281.6 6.5 %finish.1 = (f32[1,384,1280]{2,1,0:T(8,128)}, f32[1,384,1280]{2,1,0:T(8,128)}, f32[80,3840]{1,0:T(8,128)}, f32[80,1280]{1,0:T(8,128)}, f32[80,5120]{1,0:T(8,128)...) custom-call(f32[384,1280]{1,0:T(8,128)} %get-tuple-element.44.raw_ou, ...), custom_call_target="tpu_custom_call" | custom-call | tf_op jit(solution)/shard_map/finish/pallas_call | solution.py:1425

commit v3 on v2

--- a/solution.py
+++ b/solution.py
@@ -267,55 +267,74 @@
     (),
     (),
     (),
-    ((3, 0, 1, 0), (4, 0, 0), (4, 1, 0), (3, 0, 0, 0), (0, 2), (3, 1, 1, 0), (4, 0, 2), (3, 1, 0, 0), (4, 0, 1), (3, 0, 2, 0), (4, 1, 2), (4, 1, 1), (3, 2, 1, 0), (2, 4),),
-    (),
-    (),
-    ((4, 0, 3), (3, 2, 0, 0), (0, 3), (4, 2, 2), (3, 1, 2, 0), (1, 2), (4, 2, 1), (3, 2, 2, 0), (1, 3), (4, 1, 3),),
-    (),
-    (),
-    ((4, 2, 0), (3, 3, 1, 0), (0, 5), (2, 5),),
-    ((4, 2, 3),),
-    (),
-    (),
-    (),
-    (),
-    (),
-    ((3, 3, 0, 0),),
-    (),
-    (),
-    ((4, 3, 0), (2, 2), (2, 3), (0, 4),),
-    (),
-    ((3, 5, 1, 0),),
-    (),
-    (),
-    (),
-    ((3, 5, 0, 0),),
-    (),
-    (),
-    ((4, 3, 2),),
-    (),
-    (),
-    (),
-    (),
-    ((3, 3, 2, 0), (1, 5), (4, 3, 1), (1, 4), (3, 4, 1, 0), (3, 4, 0, 0), (4, 3, 3), (3, 5, 2, 0),),
-    (),
-    ((4, 5, 0),),
+    ((4, 0, 0), (3, 0, 1, 0), (2, 2), (2, 3), (4, 1, 0), (3, 0, 0, 0), (3, 1, 1, 0), (4, 0, 2), (3, 1, 0, 0), (4, 0, 1), (3, 0, 2, 0), (4, 1, 2), (0, 2), (3, 1, 2, 0), (4, 1, 1),),
+    (),
+    (),
+    ((4, 0, 3), (3, 2, 1, 0), (4, 1, 3), (3, 2, 0, 0),),
+    (),
+    ((4, 2, 2), (1, 2), (0, 3),),
+    (),
+    ((4, 2, 1), (3, 2, 2, 0),),
+    (),
+    ((4, 2, 0), (1, 3), (2, 5),),
+    (),
+    (),
+    (),
+    (),
+    ((3, 3, 1, 0), (4, 2, 3),),
+    (),
+    (),
+    (),
+    (),
+    (),
+    (),
+    (),
+    (),
+    ((3, 3, 0, 0), (4, 3, 0), (0, 5),),
+    (),
+    (),
+    (),
+    (),
+    (),
+    (),
+    ((4, 3, 2), (3, 3, 2, 0), (0, 4), (2, 4), (1, 5), (3, 5, 1, 0), (4, 3, 1), (1, 4), (3, 5, 0, 0), (3, 4, 1, 0), (4, 3, 3), (3, 4, 0, 0),),
+    (),
+    ((4, 5, 0), (3, 5, 2, 0),),
+    (),
+    (),
+    ((4, 4, 0),),
     ((3, 4, 2, 0),),
     (),
-    ((4, 4, 0),),
-    (),
+    (),
+    (),
+    ((4, 4, 2),),
     ((3, 5, 1, 1),),
     (),
     (),
-    ((4, 4, 2),),
-    (),
-    ((3, 5, 0, 1),),
-    (),
-    ((4, 4, 1),),
-    ((3, 5, 2, 1), (4, 4, 3),),
+    ((3, 5, 0, 1), (4, 4, 1),),
+    (),
+    (),
+    (),
+    ((4, 4, 3),),
+    ((3, 5, 2, 1),),
+    (),
+    (),
+    (),
+    (),
+    (),
+    (),
+    (),
+    (),
+    (),
+    (),
+    (),
+    (),
+    (),
 )
 ROWS_Z, ROWS_Y = 4, 2
 PAIR = 128
+UNIT = 640
+SLOTS = 2
 
 
 def place_of():
@@ -381,12 +400,29 @@
     lax.fori_loop(blocks * part // parts, blocks * (part + 1) // parts, rows, 0)
 
 
+def z_place(z):
+    return 2 * lax.rem(z, 2) + z // 2
+
+
+def grad_chunk(target, left, right):
+    def half(j, carry):
+        value = dot_nn(left(j), right()).astype(jnp.bfloat16)
+        n = value.shape[1]
+        rows = value.shape[0] // 8
+        for block in range(8):
+            to_z, to_y, to_core = block // 4, block // 2 % 2, block % 2
+            target[to_core, to_y, 2 * to_z + j, :, :n] = value[block * rows : (block + 1) * rows]
+        return carry
+
+    lax.fori_loop(0, 2, half, 0)
+
+
 def forward_kernel(
     hidden, cot, starts, gain1, shift1, gain2, shift2, bias_in, q_in, o_in, u_in, d_in,
-    q_all, o_all, u_all, d_all, dy_all, normed_t_out, packed_out, lse_out, att_t_out, resid_out,
-    second_t_out, act_out, act_t_out, slope_out,
+    q_all, o_all, u_all, d_all, dy_all, down_sums, normed_t_out, packed_out, lse_out, att_t_out, resid_out,
+    second_t_out, act_out, slope_out,
     hid_other, normed, wq, wo, wu, packed, mask, att_part, att_own, resid, second,
-    act, act_t, slope, normed_t, att_t, second_t, lse, u_wide, q_own, o_own, u_own, d_own, cot_own, bias,
+    act, act_t, slope, normed_t, att_t, second_t, lse, u_wide, q_own, o_own, u_own, d_own, dy, bias, parts, core_in,
     local_sem, send_sem, recv_sem, x_send, x_recv,
 ):
     bf16 = jnp.bfloat16
@@ -519,12 +555,12 @@
     local(o_in, o_own, 1).start()
     local(u_in, u_wide, 2).start()
     local(d_mine, d_own, 3).start()
-    local(cot, cot_own, 4).start()
+    local(cot, dy.at[piece], 4).start()
     greet(peers)
     for copy in q_picks:
         copy.wait()
     hidden_x = to_x(hidden, hid_other, 0)
-    cot_x = to_x(cot, dy_all.at[piece], 1)
+    cot_x = to_x(cot, dy.at[piece], 1)
     local(o_in, o_own, 1).wait()
     local(d_mine, d_own, 3).wait()
     local(u_in, u_wide, 2).wait()
@@ -534,8 +570,7 @@
         local(q_own, q_all.at[me], 0).start()
         local(o_own, o_all.at[me], 1).start()
         local(d_own, d_all.at[me], 3).start()
-        local(cot, cot_own, 4).wait()
-        local(cot_own, dy_all.at[piece], 4).start()
+        local(cot, dy.at[piece], 4).wait()
 
     units_each = 2 * rows
     group = 8 * units_each
@@ -712,8 +747,7 @@
         at = half_rows(half)
         return (
             local(act.at[at], act_out.at[at], base),
-            local(act_t.at[:, at], act_t_out.at[:, at], base + 1),
-            local(slope.at[at], slope_out.at[at], base + 2),
+            local(slope.at[at], slope_out.at[at], base + 1),
         )
 
     def second_here():
@@ -724,8 +758,36 @@
         flip_second(other)
         local(second_t, second_t_out, 13).start()
 
+    def dy_here():
+        cot_x.wait_recv()
+        local(dy, dy_all, 4).start()
+
+    def grad_down(i):
+        h, at = i // 2, slice(i % 2 * UNIT, (i % 2 + 1) * UNIT)
+
+        def left(j):
+            begin = lambda block: pl.multiple_of((8 * j + block) * 2 * rows + h * rows, 16)
+            return jnp.concatenate([act_t[pl.ds(begin(block), rows), :] for block in range(8)], axis=0)
+
+        grad_chunk(parts.at[i % SLOTS], left, lambda: dy[:, :, at].reshape(length, UNIT))
+
+    sums_x = [
+        pltpu.make_async_remote_copy(
+            src_ref=parts.at[i % SLOTS, 1 - core], dst_ref=core_in.at[i], send_sem=x_send.at[4 + pairs + i],
+            recv_sem=x_recv.at[4 + pairs + i], device_id=peers[4], device_id_type=MESH,
+        )
+        for i in range(4)
+    ]
+
+    def sum_down(i):
+        core_in[i] += parts[i % SLOTS, core]
+        sums_x[i].wait_send()
+        local(core_in.at[i], down_sums.at[i], 50 + i).start()
+
     def outputs():
-        local(cot_own, dy_all.at[piece], 4).wait()
+        for i in range(4):
+            local(core_in.at[i], down_sums.at[i], 50 + i).wait()
+        local(dy, dy_all, 4).wait()
         local(d_own, d_all.at[me], 3).wait()
         local(normed_t, normed_t_out, 8).wait()
         local(packed, packed_out, 9).wait()
@@ -754,7 +816,12 @@
     steps += [act_now(expand, piece, i) for i in range(5)]
     steps += [second_here, flip_last]
     steps += [act_now(expand, other, i) for i in range(5)]
-    steps += [outputs, act_now(all_here, (4, 5))]
+    steps += [dy_here]
+    for i in range(4):
+        steps += [act_now(grad_down, i), sums_x[i].start]
+        if i:
+            steps += [sums_x[i - 1].wait_recv, act_now(sum_down, i - 1)]
+    steps += [sums_x[3].wait_recv, act_now(sum_down, 3), outputs, act_now(all_here, (4, 5))]
     moves = (
         lambda w: pass_on(w, 0),
         lambda w: to_y(w, z, True).start(),
@@ -768,7 +835,6 @@
         step()
         if i == 1:
             first_copies()
-    cot_x.wait_recv()
     for w in range(len(own)):
         all_gone(w)
     for copy in [hidden_x, cot_x] + second_x + att_x:
@@ -790,6 +856,7 @@
         ((shards, rows, units), bf16),
         ((shards, down.shape[0] // 2, width), bf16),
         ((2, own_rows, width), bf16),
+        ((4, 2, ROWS_Z, rows, UNIT), bf16),
         ((width, length), bf16),
         ((length, cols), bf16),
         ((head_rows, length), f32),
@@ -797,7 +864,6 @@
         ((own_rows, width), f32),
         ((width, length), bf16),
         ((length, units), bf16),
-        ((units, length), bf16),
         ((length, units), bf16),
     ]
     scratch = [
@@ -824,21 +890,23 @@
         ((rows, width), bf16),
         ((rows, units), bf16),
         ((2 * rows, width), bf16),
-        ((own_rows, width), bf16),
+        ((2, own_rows, width), bf16),
         ((1, units), f32),
+        ((SLOTS, 2, 2, ROWS_Z, rows, UNIT), bf16),
+        ((4, 2, ROWS_Z, rows, UNIT), bf16),
     ]
     vmem = pl.BlockSpec(memory_space=pltpu.VMEM)
     anywhere = pl.BlockSpec(memory_space=pl.ANY)
     smem = pl.BlockSpec(memory_space=pltpu.SMEM)
     dma = pltpu.SemaphoreType.DMA
-    x_copies = 4 + cols // (3 * PAIR)
+    x_copies = 8 + cols // (3 * PAIR)
     return pl.pallas_call(
         forward_kernel,
         out_shape=[jax.ShapeDtypeStruct(shape, kind) for shape, kind in outs],
         in_specs=[vmem, anywhere, smem] + [vmem] * 5 + [anywhere] * 4,
         out_specs=[anywhere] * len(outs),
         scratch_shapes=[pltpu.VMEM(shape, kind) for shape, kind in scratch]
-        + [dma((50,)), dma((108,)), dma((108,)), dma((x_copies,)), dma((x_copies,))],
+        + [dma((54,)), dma((108,)), dma((108,)), dma((x_copies,)), dma((x_copies,))],
         compiler_params=pltpu.CompilerParams(
             collective_id=1, has_side_effects=True, vmem_limit_bytes=60 * 1024 * 1024
         ),
@@ -846,8 +914,77 @@
     )(hidden, cot, starts, gain1, shift1, gain2, shift2, bias, qkv, out, up, down)
 
 
-UNIT = 640
-SLOTS = 2
+BACKWARD_MOVES = (
+    ((2, 0), (3, 0), (1, 0), (0, 0),),
+    (),
+    (),
+    (),
+    (),
+    (),
+    (),
+    ((2, 1), (1, 1),),
+    (),
+    (),
+    (),
+    ((4, 0), (5, 0), (0, 1), (3, 1),),
+    (),
+    ((2, 2),),
+    (),
+    ((1, 2), (6, 0), (7, 0), (4, 1), (0, 2),),
+    (),
+    (),
+    (),
+    ((3, 2),),
+    ((5, 1),),
+    (),
+    (),
+    (),
+    (),
+    ((2, 3), (1, 3),),
+    (),
+    (),
+    (),
+    ((4, 2),),
+    (),
+    ((8, 0), (3, 3),),
+    ((9, 0), (6, 1),),
+    ((5, 2),),
+    ((4, 3),),
+    (),
+    (),
+    ((10, 0), (6, 2), (7, 1),),
+    ((0, 3), (5, 3),),
+    ((6, 3),),
+    (),
+    (),
+    ((11, 0), (7, 2),),
+    (),
+    ((8, 1),),
+    ((7, 3),),
+    (),
+    ((12, 0),),
+    ((8, 2),),
+    ((9, 1),),
+    (),
+    ((8, 3),),
+    (),
+    ((10, 1), (9, 2),),
+    (),
+    (),
+    (),
+    (),
+    ((10, 2), (11, 1),),
+    ((9, 3), (13, 0), (10, 3),),
+    (),
+    (),
+    ((14, 0), (12, 1), (11, 2), (13, 1), (12, 2), (11, 3),),
+    ((14, 1), (13, 2), (12, 3), (14, 2), (13, 3), (14, 3),),
+    (),
+    (),
+    (),
+    (),
+    (),
+)
 
 
 def norm_back(values, gain, grad):
@@ -864,12 +1001,12 @@
 
 
 def backward_kernel(
-    starts, gain1, gain2, hidden, dy_all, q_all, o_all, u_all, d_all, normed_t, packed, lse_in, att_t,
-    resid, second_t, act, act_t, slope,
+    starts, gain1, gain2, hidden, dy_all, q_all, o_all, u_all, d_all, down_sums, normed_t, packed, lse_in, att_t_in,
+    resid, second_t, act, slope,
     output, grad_hidden, units_out, pairs_out, small_out,
-    lhs, half_act, wide, wd, wu, dy, first, second, d_att, x_in0, x_in1, x_out0, x_out1,
-    down_own, parts, core_in, core_in_q, y_in, y_in_q, z_in, z_in_q, lse, acc_k, acc_v,
-    bias_sum, small, small_core, small_y, small_z,
+    lhs, att_t, half_act, wide, wd, wu, dy, first, second, d_att, x_in0, x_in1, x_out0, down_own,
+    parts, core_in, core_in_q, y_in, y_in_q, z_in, z_in_q, lse, acc_k, acc_v, bias_sum, early, late,
+    early_near, late_near, early_all, late_all, small,
     local_sem, a_send, a_recv, b_send, b_recv, c_send, c_recv, g_send, g_recv, x_send, x_recv,
     s_send, s_recv, keep_sem,
 ):
@@ -881,12 +1018,24 @@
     length = 2 * own_rows
     branch = half_act.at[:, pl.ds(0, width)]
     units = wide.shape[1]
-    cols = 3 * d_att.shape[1]
-    pairs = d_att.shape[1] // PAIR
-    peers = neighbours()
+    d_width = d_att.shape[1]
+    cols = 3 * d_width
+    pairs = d_width // PAIR
+    near = z + 1 - 2 * lax.rem(z, 2)
+    far = lax.rem(z + 2, ROWS_Z)
+    peer_core, peer_y = {"rows": row_of(z, y, 1 - core)}, {"rows": row_of(z, 1 - y, core)}
+    peer_near, peer_far = {"rows": row_of(near, y, core)}, {"rows": row_of(far, y, core)}
+    peer_x = {"blk": other}
+    group = [peer_core, peer_y, {"rows": row_of(z, 1 - y, 1 - core)}]
+    line = [
+        {"rows": row_of(z + k, y, core), "blk": lax.rem(piece + n, 2)} for n in range(2) for k in range(ROWS_Z) if n or k
+    ]
     wide_chunks = core_in.shape[0]
+    chunks = wide_chunks + pairs
     first_gain, second_gain = gain1[...].reshape(1, width), gain2[...].reshape(1, width)
     half_rows = lambda half: pl.ds(pl.multiple_of(half * own_rows, 128), own_rows)
+    part_rows = own_rows // 2
+    part_at = lambda part: pl.ds(part * part_rows, part_rows)
 
     def remote(src, dst, sends, recvs, index, peer):
         return pltpu.make_async_remote_copy(
@@ -895,7 +1044,7 @@
         )
 
     loads = {
-        "act_t": (act_t, lhs, 0),
+        "sums": (down_sums, core_in.at[pl.ds(0, 4)], 0),
         "dy": (dy_all, dy, 1),
         "down": (d_all, wd, 2),
         "slope": (slope, wide, 3),
@@ -904,8 +1053,8 @@
         "act_own": (act.at[half_rows(piece)], half_act, 6),
         "resid": (resid, second, 7),
         "lse": (lse_in, lse, 8),
-        "second_t": (second_t, lhs.at[:, pl.ds(0, lhs.shape[1] // 2)], 9),
-        "att_t": (att_t, lhs.at[:, pl.ds(lhs.shape[1] // 2, lhs.shape[1] // 2), pl.ds(0, own_rows)], 10),
+        "second_t": (second_t, lhs, 9),
+        "att_t": (att_t_in, att_t, 10),
         "out": (o_all, wd.at[pl.ds(0, width)], 11),
         "normed_t": (normed_t, wd.at[pl.ds(width, width), pl.ds(0, length)], 12),
         "qkv": (q_all, wu.at[:, pl.ds(0, cols)], 13),
@@ -919,142 +1068,151 @@
         src, dst, index = loads[name]
         return pltpu.make_async_copy(src, dst, local_sem.at[index])
 
+    z_first = (0, 1)
+    mine, theirs = pl.ds(2 * lax.rem(z, 2), 2), pl.ds(2 - 2 * lax.rem(z, 2), 2)
+    place, far_place = z_place(z), z_place(far)
+    order = tuple(range(chunks))
+
     def buffers(i):
         if i < wide_chunks:
-            return core_in.at[i], y_in.at[i], z_in.at[i], z_in.at[i, 0], units_out.at[:, i], UNIT
+            return core_in.at[i], y_in.at[i], z_in.at[i], units_out.at[:, i], UNIT
         i -= wide_chunks
-        return core_in_q.at[i], y_in_q.at[i], z_in_q.at[i], z_in_q.at[i, 0], pairs_out.at[:, i], 3 * PAIR
+        return core_in_q.at[i], y_in_q.at[i], z_in_q.at[i], pairs_out.at[:, i], 3 * PAIR
 
     def copy_a(i):
-        into, _, _, _, _, n = buffers(i)
-        return remote(parts.at[i % SLOTS, 1 - core, :, :, :, pl.ds(0, n)], into, a_send, a_recv, i, peers[4])
+        into, _, _, _, n = buffers(i)
+        return remote(parts.at[i % SLOTS, 1 - core, :, :, :, pl.ds(0, n)], into, a_send, a_recv, i, peer_core)
 
     def copy_b(i):
-        sums, into, _, _, _, _ = buffers(i)
-        return remote(sums.at[1 - y], into, b_send, b_recv, i, peers[3])
-
-    def copy_c(i, k):
-        _, sums, into, _, _, _ = buffers(i)
-        return remote(sums.at[lax.rem(z + k, ROWS_Z)], into.at[k - 1], c_send, c_recv, 3 * i + k - 1, peers[k - 1])
+        sums, by_y, by_z, _, _ = buffers(i)
+        if i in z_first:
+            return remote(sums.at[1 - y, place], by_z.at[2], b_send, b_recv, i, peer_y)
+        return remote(sums.at[1 - y], by_y, b_send, b_recv, i, peer_y)
+
+    def copies_c(i, step):
+        sums, by_y, by_z, _, _ = buffers(i)
+        index = 4 * i + 2 * step
+        if i not in z_first:
+            if step == 0:
+                return [remote(by_y.at[theirs], by_z.at[pl.ds(0, 2)], c_send, c_recv, index, peer_near)]
+            return [remote(by_y.at[far_place], by_z.at[2], c_send, c_recv, index, peer_far)]
+        if step == 0:
+            return [
+                remote(sums.at[v, theirs], by_y.at[pl.ds(2 * v, 2)], c_send, c_recv, index + v, peer_near)
+                for v in range(2)
+            ]
+        return [remote(sums.at[v, far_place], by_z.at[v], c_send, c_recv, index + v, peer_far) for v in range(2)]
 
     def copy_g(i):
-        _, _, _, share, out, _ = buffers(i)
-        return remote(share, out.at[piece], g_send, g_recv, i, peers[5])
+        _, _, by_z, out, _ = buffers(i)
+        return remote(by_z.at[0], out.at[piece], g_send, g_recv, i, peer_x)
 
     def keep_g(i):
-        _, _, _, share, out, _ = buffers(i)
-        return pltpu.make_async_copy(share, out.at[piece], keep_sem.at[i])
-
-    def finish_a(i):
-        sums, _, _, _, _, n = buffers(i)
-        copy_a(i).wait_recv()
-        slot = i % SLOTS
-        sums[1 - y] += parts[slot, core, 1 - y, :, :, :n]
-        copy_b(i).start()
-        sums[y] += parts[slot, core, y, :, :, :n]
-        copy_a(i).wait_send()
-
-    def finish_b(i):
-        mine, sums, _, _, _, _ = buffers(i)
-        copy_b(i).wait_recv()
-        sums[...] += mine[y]
-        for k in (1, 3, 2):
-            copy_c(i, k).start()
-
-    def finish_c(i):
-        _, sums, terms, share, _, _ = buffers(i)
-        for k in (1, 3, 2):
-            copy_c(i, k).wait_recv()
-        total = sums[z].astype(f32)
-        for k in range(3):
-            total += terms[k].astype(f32)
-        share[...] = total.astype(bf16)
-        copy_g(i).start()
-        keep_g(i).start()
-
-    def grad_chunk(i, left, right):
-        slot = i % SLOTS
-
-        def one_z(to_z, carry):
-            value = dot_nn(left(to_z), right()).astype(bf16)
-            n = value.shape[1]
-            rows = value.shape[0] // 4
-            for block in range(4):
-                to_y, to_core = divmod(block, 2)
-                parts[slot, to_core, to_y, to_z, :, :n] = value[block * rows : (block + 1) * rows]
-            return carry
-
-        lax.fori_loop(0, ROWS_Z, one_z, 0)
-        copy_a(i).start()
-
-    for name in ("act_t", "dy", "down", "slope", "act_other", "up", "resid", "lse"):
+        _, _, by_z, out, _ = buffers(i)
+        return pltpu.make_async_copy(by_z.at[0], out.at[piece], keep_sem.at[i])
+
+    def move(i, stage):
+        sums, by_y, by_z, _, n = buffers(i)
+        if stage == 0:
+            slot = i % SLOTS
+            if i >= 4:
+                copy_a(i).wait_recv()
+                sums[1 - y] += parts[slot, core, 1 - y, :, :, :n]
+            if i in z_first:
+                for copy in copies_c(i, 0):
+                    copy.start()
+            else:
+                copy_b(i).start()
+            if i >= 4:
+                sums[y] += parts[slot, core, y, :, :, :n]
+                copy_a(i).wait_send()
+        elif i in z_first and stage < 3:
+            for v, copy in enumerate(copies_c(i, stage - 1)):
+                copy.wait_recv()
+                if stage == 1:
+                    sums[v, mine] += by_y[2 * v : 2 * v + 2]
+                else:
+                    sums[v, place] += by_z[v]
+            for copy in copies_c(i, 1) if stage == 1 else [copy_b(i)]:
+                copy.start()
+        elif stage == 1:
+            copy_b(i).wait_recv()
+            by_y[...] += sums[y]
+            copies_c(i, 0)[0].start()
+        elif stage == 2:
+            copies_c(i, 0)[0].wait_recv()
+            by_y[mine] += by_z[0:2]
+            copies_c(i, 1)[0].start()
+        else:
+            if i in z_first:
+                copy_b(i).wait_recv()
+                total = sums[y, place].astype(f32) + by_z[2].astype(f32)
+            else:
+                copies_c(i, 1)[0].wait_recv()
+                total = by_y[place].astype(f32) + by_z[2].astype(f32)
+            by_z[0] = total.astype(bf16)
+            copy_g(i).start()
+            keep_g(i).start()
+
+    for name in ("sums", "dy", "down", "slope", "up", "act_other", "second_t", "resid", "lse", "att_t"):
         local(name).start()
-    greet(peers)
-    local("act_t").wait()
-    local("dy").wait()
-    block_rows = parts.shape[4]
-
-    def grad_down(i):
-        h, column = divmod(i, 2)
-
-        def left(to_z):
-            rows = lhs[pl.ds(to_z * 4, 4), h * block_rows : (h + 1) * block_rows, :]
-            return rows.reshape(4 * block_rows, length)
-
-        grad_chunk(i, left, lambda: dy[:, :, column * UNIT : (column + 1) * UNIT].reshape(length, UNIT))
-
-    grad_down(0)
-    grad_down(1)
-    finish_a(0)
-    grad_down(2)
-    finish_a(1)
-    grad_down(3)
-    local("second_t").start()
-    local("att_t").start()
-    local("down").wait()
-    local("slope").wait()
+    greet(group + line)
+    local("sums").wait()
+
+    def ready_units():
+        for name in ("dy", "down", "slope"):
+            local(name).wait()
 
     tile = 256
 
-    def d_units(i, carry):
-        at = aligned(i, tile)
-        sums = jnp.zeros((1, tile), f32)
-        for half in range(2):
-            rows = slice(half * own_rows, (half + 1) * own_rows)
-            value = dot_nt(dy[half], wd[at, :]) * wide[rows, at].astype(f32)
-            low = value.astype(bf16)
-            wide[rows, at] = low
-            sums += jnp.sum(low.astype(f32), axis=0, keepdims=True)
-        bias_sum[:, at] = sums
-        return carry
-
-    lax.fori_loop(0, 4, d_units, 0)
-    finish_a(2)
-    finish_a(3)
-    lax.fori_loop(4, units // tile, d_units, 0)
-    local("up").wait()
-
-    def d_second(half, write):
+    def d_units(begin, end):
         def body(i, carry):
             at = aligned(i, tile)
-            write(at, dot_nt(wide[half_rows(half), :], wu[at, :]))
+            value = dot_nt(dy[...].reshape(length, width), wd[at, :]) * wide[:, at].astype(f32)
+            low = value.astype(bf16)
+            wide[:, at] = low
+            bias_sum[:, at] = jnp.sum(low.astype(f32), axis=0, keepdims=True)
             return carry
 
+        lax.fori_loop(begin, end, body, 0)
+
+    def times_up(rows, write):
+        def body(i, carry):
+            at = aligned(i, tile)
+            write(at, dot_nt(wide[rows, :], wu[at, :]))
+            return carry
+
         lax.fori_loop(0, width // tile, body, 0)
 
-    def write_out0(at, value):
-        x_out0[:, at] = value.astype(bf16)
-
-    def write_first(at, value):
-        first[:, at] = value
-
-    d_second(other, write_out0)
-    second_x = remote(x_out0, x_in0, x_send, x_recv, 0, peers[5])
-    second_x.start()
-    d_second(piece, write_first)
-    local("qkv").start()
-    finish_b(0)
-    local("act_other").wait()
+    def d_second_other(part):
+        if part == 0:
+            local("up").wait()
+
+        def write(at, value):
+            x_out0[part_at(part), at] = value.astype(bf16)
+
+        times_up(pl.ds(pl.multiple_of(other * own_rows + part * part_rows, 64), part_rows), write)
+
+    def exchange(part, index):
+        return remote(x_out0.at[part_at(part)], x_in0.at[part_at(part)], x_send, x_recv, index, peer_x)
+
+    second_x = [exchange(part, part) for part in range(2)]
+    normed_x = [exchange(part, 2 + part) for part in range(2)]
+    down_x = remote(dy.at[other], x_in1, x_send, x_recv, 4, peer_x)
+    att_x = [
+        remote(
+            x_out0.at[:, pl.ds(p * PAIR, PAIR)], d_att.at[half_rows(piece), pl.ds(p * PAIR, PAIR)],
+            x_send, x_recv, 5 + p, peer_x,
+        )
+        for p in range(pairs)
+    ]
+
+    def d_second_own():
+        def write(at, value):
+            first[:, at] = value
+
+        times_up(half_rows(piece), write)
+        local("qkv").start()
 
     def down_part(target):
         def body(i, carry):
@@ -1064,134 +1222,121 @@
 
         lax.fori_loop(0, width // tile, body, 0)
 
-    down_part(x_out1)
-    local("act_own").start()
-    local("second_t").wait()
+    def down_other():
+        local("act_other").wait()
+        down_part(dy.at[other])
+        local("act_own").start()
+
+    def down_mine():
+        local("act_own").wait()
+        down_part(down_own)
+        local("out").start()
+        local("normed_t").start()
+
+    def chunk(i, left, right):
+        grad_chunk(parts.at[i % SLOTS], left, right)
+        copy_a(i).start()
 
     def grad_up(i):
-        def left(to_z):
-            rows = lhs[pl.ds(to_z * 4, 4), :block_rows, :]
-            return rows.reshape(4 * block_rows, length)
-
-        grad_chunk(4 + i, left, lambda: wide[:, i * UNIT : (i + 1) * UNIT])
-
-    grad_up(0)
-    grad_up(1)
-    local("act_own").wait()
-    finish_a(4)
-    finish_b(1)
-    down_part(down_own)
-    local("out").start()
-    local("normed_t").start()
-    finish_a(5)
-    grad_up(2)
-    grad_up(3)
-    local("packed").start()
+        if i == 0:
+            local("second_t").wait()
+        left = lambda j: lhs[pl.ds(8 * j, 8)].reshape(8 * lhs.shape[1], length)
+        chunk(4 + i, left, lambda: wide[:, i * UNIT : (i + 1) * UNIT])
+        if i == 3:
+            local("packed").start()
+
     mask = lhs.at[:, pl.ds(0, length // lhs.shape[0]), :]
-    write_mask(starts, mask)
-    finish_a(6)
-    finish_a(7)
-    finish_c(0)
-    finish_b(2)
-    local("resid").wait()
-    second_x.wait_recv()
     step = 64
 
-    def back_two(i, carry):
-        rows = aligned(i, step)
-        grad = first[rows, :] + x_in0[rows, :].astype(f32)
-        d_values, d_gain, d_shift = norm_back(second[rows, :], second_gain, grad)
-        total = dy[piece, rows, :].astype(f32) + d_values
-        first[rows, :] = total
-        branch[rows, :] = total.astype(bf16)
-        return carry[0] + d_gain, carry[1] + d_shift
-
-    zeros = jnp.zeros((1, width), f32)
-    gain_two, shift_two = lax.fori_loop(0, own_rows // step, back_two, (zeros, zeros))
-    small[2:3, :] = gain_two
-    small[3:4, :] = shift_two
-    local("out").wait()
-    second_x.wait_send()
-    d_width = d_att.shape[1]
+    def back_two(part):
+        if part == 0:
+            local("resid").wait()
+        second_x[part].wait_recv()
+
+        def body(i, carry):
+            rows = aligned(i, step)
+            grad = first[rows, :] + x_in0[rows, :].astype(f32)
+            d_values, d_gain, d_shift = norm_back(second[rows, :], second_gain, grad)
+            total = dy[piece, rows, :].astype(f32) + d_values
+            first[rows, :] = total
+            branch[rows, :] = total.astype(bf16)
+            early[0:1, :] += d_gain
+            early[1:2, :] += d_shift
+            return carry
+
+        steps_each = part_rows // step
+        if part == 0:
+            early[...] = jnp.zeros_like(early)
+        lax.fori_loop(part * steps_each, (part + 1) * steps_each, body, 0)
 
     def d_attended(half):
         rows = pl.ds(pl.multiple_of(half * d_width, 128), d_width)
         return dot_nt(branch[...], wd[rows, :]).astype(bf16)
 
-    x_out0[:, :d_width] = d_attended(other)
-    att_x = remote(x_out0.at[:, pl.ds(0, d_width)], d_att.at[half_rows(piece)], x_send, x_recv, 1, peers[5])
-    att_x.start()
-    down_x = remote(x_out1, x_in1, x_send, x_recv, 2, peers[5])
-    down_x.start()
-    d_att[half_rows(piece), :] = d_attended(piece)
-    local("att_t").wait()
+    def d_att_other():
+        local("out").wait()
+        for copy in second_x:
+            copy.wait_send()
+        x_out0[:, :d_width] = d_attended(other)
+
+    def d_att_own():
+        d_att[half_rows(piece), :] = d_attended(piece)
 
     def grad_out(i):
-        def left(to_z):
-            rows = lhs[pl.ds(to_z * 4, 4), block_rows : 2 * block_rows, :own_rows]
-            return rows.reshape(4 * block_rows, own_rows)
-
-        grad_chunk(8 + i, left, lambda: branch[:, i * UNIT : (i + 1) * UNIT])
-
-    grad_out(0)
-    grad_out(1)
-    finish_c(1)
-    finish_b(3)
-    finish_a(8)
-    finish_a(9)
-    local("hidden").start()
-    local("lse").wait()
-    local("packed").wait()
-    local("normed_t").wait()
-    att_x.wait_recv()
+        if i == 0:
+            local("att_t").wait()
+        left = lambda j: att_t[pl.ds(8 * j, 8)].reshape(8 * att_t.shape[1], own_rows)
+        chunk(8 + i, left, lambda: branch[:, i * UNIT : (i + 1) * UNIT])
+        if i == 1:
+            local("hidden").start()
+
     first_lanes = head_lanes(PAIR)
+    query_chunk = 256
 
     def pair_cols(p):
         return tuple(slice(t * d_width + PAIR * p, t * d_width + PAIR * (p + 1)) for t in range(3))
 
-    def attend_back(p):
+    def att_here(p):
+        if p == 0:
+            for name in ("lse", "packed", "normed_t"):
+                local(name).wait()
+        att_x[p].wait_recv()
+        acc_k[...] = jnp.zeros_like(acc_k)
+        acc_v[...] = jnp.zeros_like(acc_v)
+
+    def attend_back(p, i):
         at_q, at_k, at_v = pair_cols(p)
         keys_t = wide[:, at_k].T
-        acc_k[...] = jnp.zeros_like(acc_k)
-        acc_v[...] = jnp.zeros_like(acc_v)
-        chunk = 256
-
-        def body(i, carry):
-            rows = aligned(i, chunk)
-            keys = wide[:, at_k]
-            values = wide[:, at_v]
-            queries = wide[rows, at_q]
-            grads = d_att[rows, p * PAIR : (p + 1) * PAIR]
-            blocked = mask[:, :, rows].reshape(length, chunk).astype(f32)
-            parts_q = []
-            for h in range(2):
-                one_q = jnp.where(first_lanes[h], queries, jnp.zeros_like(queries))
-                one_g = jnp.where(first_lanes[h], grads, jnp.zeros_like(grads))
-                scores = dot_nt(keys, one_q) + (blocked - lse[2 * p + h : 2 * p + h + 1, rows])
-                probs = jnp.exp(scores)
-                d_probs = dot_nt(values, one_g)
-                dots = jnp.sum(probs * d_probs, axis=0, keepdims=True)
-                d_scores = (probs * (d_probs - dots)).astype(bf16)
-                acc_v[...] += dot_nn(probs.astype(bf16), one_g)
-                acc_k[...] += dot_nn(d_scores, one_q)
-                parts_q.append(dot_nn(keys_t[h * HEAD_DIM : (h + 1) * HEAD_DIM], d_scores))
-            d_queries = jnp.concatenate(parts_q, axis=0).T * HEAD_DIM ** (-0.5)
-            wide[rows, at_q] = d_queries.astype(bf16)
-            return carry
-
-        lax.fori_loop(0, length // chunk, body, 0)
-        wide[:, at_k] = acc_k[...].astype(bf16)
-        wide[:, at_v] = acc_v[...].astype(bf16)
+        rows = slice(i * query_chunk, (i + 1) * query_chunk)
+        keys = wide[:, at_k]
+        values = wide[:, at_v]
+        queries = wide[rows, at_q]
+        grads = d_att[rows, p * PAIR : (p + 1) * PAIR]
+        blocked = mask[:, :, rows].reshape(length, query_chunk).astype(f32)
+        parts_q = []
+        for h in range(2):
+            one_q = jnp.where(first_lanes[h], queries, jnp.zeros_like(queries))
+            one_g = jnp.where(first_lanes[h], grads, jnp.zeros_like(grads))
+            scores = dot_nt(keys, one_q) + (blocked - lse[2 * p + h : 2 * p + h + 1, rows])
+            probs = jnp.exp(scores)
+            d_probs = dot_nt(values, one_g)
+            dots = jnp.sum(probs * d_probs, axis=0, keepdims=True)
+            d_scores = (probs * (d_probs - dots)).astype(bf16)
+            acc_v[...] += dot_nn(probs.astype(bf16), one_g)
+            acc_k[...] += dot_nn(d_scores, one_q)
+            parts_q.append(dot_nn(keys_t[h * HEAD_DIM : (h + 1) * HEAD_DIM], d_scores))
+        d_queries = jnp.concatenate(parts_q, axis=0).T * HEAD_DIM ** (-0.5)
+        wide[rows, at_q] = d_queries.astype(bf16)
+        if i == length // query_chunk - 1:
+            wide[:, at_k] = acc_k[...].astype(bf16)
+            wide[:, at_v] = acc_v[...].astype(bf16)
 
     def grad_pair(p):
-        def left(to_z):
-            return wd[pl.ds(pl.multiple_of(width + to_z * 4 * block_rows, 64), 4 * block_rows), :length]
-
-        grad_chunk(10 + p, left, lambda: jnp.concatenate([wide[:, at] for at in pair_cols(p)], axis=1))
+        n = 8 * parts.shape[4]
+        left = lambda j: wd[pl.ds(pl.multiple_of(width + j * n, 64), n), :length]
+        chunk(10 + p, left, lambda: jnp.concatenate([wide[:, at] for at in pair_cols(p)], axis=1))
 
     def write_output():
-        down_x.wait_recv()
-
         def body(i, carry):
             rows = aligned(i, step)
             second[rows, :] += down_own[rows, :].astype(f32) + x_in1[rows, :].astype(f32)
@@ -1200,97 +1345,129 @@
         lax.fori_loop(0, own_rows // step, body, 0)
         local("output").start()
 
-    ticks = {
-        0: lambda: (finish_c(2), finish_b(4)),
-        1: lambda: (finish_a(10), finish_c(3), finish_b(5)),
-        2: lambda: (finish_a(11), finish_c(4), finish_b(6)),
-        3: lambda: (finish_a(12), write_output(), finish_c(5), finish_b(7)),
-        4: lambda: (finish_a(13), finish_c(6)),
-    }
-    for p in range(pairs):
-        attend_back(p)
-        grad_pair(p)
-        ticks[p]()
-    finish_a(14)
-    local("qkv").wait()
-    local("output").wait()
-    att_x.wait_send()
-
-    def d_normed(half, write):
+    def times_qkv(rows, write):
         def body(i, carry):
             at = aligned(i, tile)
-            write(at, dot_nt(wide[half_rows(half), :cols], wu[at, :cols]))
+            write(at, dot_nt(wide[rows, :cols], wu[at, :cols]))
             return carry
 
         lax.fori_loop(0, width // tile, body, 0)
 
-    def write_second(at, value):
-        second[:, at] = value
-
-    d_normed(other, write_out0)
-    normed_x = remote(x_out0, x_in0, x_send, x_recv, 3, peers[5])
-    normed_x.start()
-    finish_b(8)
-    d_normed(piece, write_second)
-    finish_c(7)
-    finish_b(9)
-    local("hidden").wait()
-    finish_c(8)
-    finish_b(10)
-    normed_x.wait_recv()
-
-    def back_one(i, carry):
-        rows = aligned(i, step)
-        grad = second[rows, :] + x_in0[rows, :].astype(f32)
-        d_values, d_gain, d_shift = norm_back(branch[rows, :].astype(f32), first_gain, grad)
-        first[rows, :] += d_values
-        return carry[0] + d_gain, carry[1] + d_shift
-
-    gain_one, shift_one = lax.fori_loop(0, own_rows // step, back_one, (zeros, zeros))
-    local("grad_hidden").start()
-    small[0:1, :] = gain_one
-    small[1:2, :] = shift_one
-    small[4:5, :] = bias_sum[:, :width]
-    small[5:6, :] = bias_sum[:, width:]
-    small[6:8, :] = jnp.zeros((2, width), f32)
-    core_x = remote(small, small_core, s_send, s_recv, 0, peers[4])
-    core_x.start()
-    finish_b(11)
-    core_x.wait()
-    small[...] += small_core[...]
-    y_x = remote(small, small_y, s_send, s_recv, 1, peers[3])
-    y_x.start()
-    finish_c(9)
-    finish_b(12)
-    finish_c(10)
-    finish_b(13)
-    finish_c(11)
-    finish_b(14)
-    y_x.wait()
-    small_z[z] = small[...] + small_y[...]
-    z_x = [remote(small_z.at[z], small_z.at[z], s_send, s_recv, 1 + k, peers[k - 1]) for k in (1, 2, 3)]
-    for copy in z_x:
-        copy.start()
-    finish_c(12)
-    finish_c(13)
-    for copy in z_x:
-        copy.wait()
-    small[...] = ((small_z[0] + small_z[1]) + small_z[2]) + small_z[3]
-    share_x = remote(small, small_out.at[piece], s_send, s_recv, 5, peers[5])
-    share_x.start()
-    share_keep = pltpu.make_async_copy(small, small_out.at[piece], keep_sem.at[15])
-    share_keep.start()
-    finish_c(14)
-    for i in range(15):
+    def d_normed_other(part):
+        if part == 0:
+            local("qkv").wait()
+            for copy in att_x:
+                copy.wait_send()
+
+        def write(at, value):
+            x_out0[part_at(part), at] = value.astype(bf16)
+
+        times_qkv(pl.ds(pl.multiple_of(other * own_rows + part * part_rows, 64), part_rows), write)
+
+    def d_normed_own():
+        local("output").wait()
+
+        def write(at, value):
+            second[:, at] = value
+
+        times_qkv(half_rows(piece), write)
+
+    def back_one(part):
+        if part == 0:
+            local("hidden").wait()
+            late[...] = jnp.zeros_like(late)
+        normed_x[part].wait_recv()
+
+        def body(i, carry):
+            rows = aligned(i, step)
+            grad = second[rows, :] + x_in0[rows, :].astype(f32)
+            d_values, d_gain, d_shift = norm_back(branch[rows, :].astype(f32), first_gain, grad)
+            first[rows, :] += d_values
+            late[0:1, :] += d_gain
+            late[1:2, :] += d_shift
+            return carry
+
+        steps_each = part_rows // step
+        lax.fori_loop(part * steps_each, (part + 1) * steps_each, body, 0)
+        if part == 1:
+            local("grad_hidden").start()
+
+    def small_near(value, near_slots, base):
+        own_slot = 2 * y + core
+        return [
+            remote(value, near_slots.at[own_slot], s_send, s_recv, base + k, peer) for k, peer in enumerate(group)
+        ]
+
+    def small_line(all_slots, base):
+        own_slot = z * 2 + piece
+        return [
+            remote(all_slots.at[own_slot], all_slots.at[own_slot], s_send, s_recv, base + 3 + k, peer)
+            for k, peer in enumerate(line)
+        ]
+
+    def small_one(value, near_slots, base):
+        near_slots[2 * y + core] = value[...]
+        for copy in small_near(value, near_slots, base):
+            copy.start()
+
+    def small_two(value, near_slots, all_slots, base):
+        for copy in small_near(value, near_slots, base):
+            copy.wait()
+        all_slots[z * 2 + piece] = ((near_slots[0] + near_slots[1]) + near_slots[2]) + near_slots[3]
+        for copy in small_line(all_slots, base):
+            copy.start()
+
+    def small_three(all_slots, base, at):
+        for copy in small_line(all_slots, base):
+            copy.wait()
+        n = all_slots.shape[1]
+        for x in range(2):
+            total = ((all_slots[x] + all_slots[2 + x]) + all_slots[4 + x]) + all_slots[6 + x]
+            small[x, at : at + n, :] = total
+
+    def early_one():
+        early[2:3, :] = bias_sum[:, :width]
+        early[3:4, :] = bias_sum[:, width:]
+        small_one(early, early_near, 0)
+
+    call = functools.partial
+    steps = [ready_units, call(d_units, 0, 3), call(d_units, 3, 6), call(d_units, 6, 10)]
+    for part in range(2):
+        steps += [call(d_second_other, part), second_x[part].start]
+    steps += [call(grad_up, 0), call(grad_up, 1), d_second_own, down_other, call(grad_up, 2), call(grad_up, 3), down_mine]
+    steps += [call(write_mask, starts, mask), call(back_two, 0), call(back_two, 1), d_att_other]
+    steps += [copy.start for copy in att_x]
+    steps += [d_att_own, down_x.start, early_one, call(grad_out, 0), call(grad_out, 1)]
+    for p in range(pairs):
+        steps += [call(att_here, p)] + [call(attend_back, p, i) for i in range(length // query_chunk)]
+        if p < 3:
+            steps += [call(grad_pair, p)]
+        if p == 1:
+            steps += [call(small_two, early, early_near, early_all, 0)]
+    for part in range(2):
+        steps += [call(d_normed_other, part), normed_x[part].start]
+    steps += [call(grad_pair, 3), call(grad_pair, 4), down_x.wait_recv, write_output, d_normed_own]
+    steps += [call(back_one, 0), call(back_one, 1), call(small_one, late, late_near, 10)]
+    steps += [call(small_three, early_all, 0, 2), call(small_two, late, late_near, late_all, 10)]
+    steps += [call(small_three, late_all, 10, 0)]
+    for i, one in enumerate(steps):
+        for where in BACKWARD_MOVES[i]:
+            move(*where)
+        one()
+    small_keep = pltpu.make_async_copy(small, small_out, keep_sem.at[chunks])
+    small_keep.start()
+    for where in BACKWARD_MOVES[len(steps)]:
+        move(*where)
+    for i in range(chunks):
         copy_b(i).wait_send()
-        for k in (1, 2, 3):
-            copy_c(i, k).wait_send()
+        for copy in copies_c(i, 0) + copies_c(i, 1):
+            copy.wait_send()
         copy_g(i).wait()
         keep_g(i).wait()
-    share_x.wait()
-    share_keep.wait()
+    small_keep.wait()
     down_x.wait_send()
-    normed_x.wait_send()
+    for copy in normed_x:
+        copy.wait_send()
     local("grad_hidden").wait()
 
 
@@ -1307,11 +1484,12 @@
         ((own_rows, width), f32),
         ((2, wide_units, rows, UNIT), bf16),
         ((2, pairs, rows, pair_cols), bf16),
-        ((2, 8, width), f32),
+        ((2, 6, width), f32),
     ]
     token = ((own_rows, width), bf16)
     scratch = [
-        ((16, 2 * rows, length), bf16),
+        ((16, rows, length), bf16),
+        ((16, rows, own_rows), bf16),
         ((own_rows, units), bf16),
         ((length, units), bf16),
         ((units, width), bf16),
@@ -1320,7 +1498,7 @@
         ((own_rows, width), f32),
         ((own_rows, width), f32),
         ((length, cols // 3), bf16),
-        token, token, token, token, token,
+        token, token, token, token,
         ((SLOTS, 2, 2, ROWS_Z, rows, UNIT), bf16),
         ((wide_units, 2, ROWS_Z, rows, UNIT), bf16),
         ((pairs, 2, ROWS_Z, rows, pair_cols), bf16),
@@ -1332,17 +1510,20 @@
         ((length, PAIR), f32),
         ((length, PAIR), f32),
         ((1, units), f32),
-        ((8, width), f32),
-        ((8, width), f32),
-        ((8, width), f32),
-        ((ROWS_Z, 8, width), f32),
+        ((4, width), f32),
+        ((2, width), f32),
+        ((4, 4, width), f32),
+        ((4, 2, width), f32),
+        ((8, 4, width), f32),
+        ((8, 2, width), f32),
+        ((2, 6, width), f32),
     ]
     vmem = pl.BlockSpec(memory_space=pltpu.VMEM)
     anywhere = pl.BlockSpec(memory_space=pl.ANY)
     smem = pl.BlockSpec(memory_space=pltpu.SMEM)
     chunks = wide_units + pairs
     dma = lambda n: pltpu.SemaphoreType.DMA((n,))
-    sems = [18] + [chunks] * 4 + [3 * chunks] * 2 + [chunks] * 2 + [4, 4, 6, 6, chunks + 1]
+    sems = [18] + [chunks] * 4 + [4 * chunks] * 2 + [chunks] * 2 + [5 + pairs] * 2 + [20, 20, chunks + 1]
     return pl.pallas_call(
         backward_kernel,
         out_shape=[jax.ShapeDtypeStruct(shape, kind) for shape, kind in outs],
@@ -1442,8 +1623,8 @@
 ):
     shards = lax.axis_size("rows")
     (
-        qkv_all, out_all, up_all, down_all, dy_all, normed_t, packed, lse, att_t, residual, second_t,
-        activated, activated_t, slope,
+        qkv_all, out_all, up_all, down_all, dy_all, down_sums, normed_t, packed, lse, att_t, residual, second_t,
+        activated, slope,
     ) = forward(
         hidden[0], cotangent[0], starts, first_gain, first_shift, second_gain, second_shift, hidden_bias,
         qkv_weight, out_weight, up_weight, down_weight,
@@ -1452,8 +1633,8 @@
     blocks = lambda w: w.reshape(shards, -1, w.shape[-1])
     shares = backward(
         starts, first_gain, second_gain, hidden[0], dy_all, whole(qkv_all), whole(out_all),
-        whole(up_all), whole(down_all), normed_t, packed, lse, blocks(att_t), residual,
-        blocks(second_t), activated, blocks(activated_t), slope,
+        whole(up_all), whole(down_all), down_sums, normed_t, packed, lse, blocks(att_t), residual,
+        blocks(second_t), activated, slope,
     )
     return tuple(finish(*shares))
 

time: 292 us -> 279 us (0.955)
  Pallas kernels: 287 us -> 275 us
    pallas_call x1, Pallas kernels: 160 us -> 139 us  [backward(): pl.pallas_call(backward_kernel, out_shape=[jax.ShapeDtypeStruct(shape, ki...]
    pallas_call x1, Pallas kernels: 121 us -> 130 us  [forward(): pl.pallas_call(forward_kernel, out_shape=[jax.ShapeDtypeStruct(shape, kin...]
where the time goes in v3:
time: 279 us; the launch traced here: 276 us
  Pallas kernels  275 us (99%)
    pallas_call x1, Pallas kernels, backward(): pl.pallas_call(backward_kernel, out_shape=[jax.ShapeDtypeStruct(shape, ki...  139 us
    pallas_call x1, Pallas kernels, forward(): pl.pallas_call(forward_kernel, out_shape=[jax.ShapeDtypeStruct(shape, kin...  130 us
    pallas_call x1, Pallas kernels, finish(): pl.pallas_call(finish_kernel, grid=(2,), out_shape=[jax.ShapeDtypeStruct(...  6.48 us

profile of v3, /device:TPU:0, one launch (start us, length us, event | category | flops | bytes accessed | tf_op | source)
XLA Modules:
  0.0 275.8 jit_solution(659591496122062301)
XLA Ops:
  0.6 129.8 %forward.1 = (bf16[16,80,1920]{2,1,0:T(8,128)(2,1)}, bf16[16,80,1280]{2,1,0:T(8,128)(2,1)}, bf16[16,80,2560]{2,1,0:T(8,128)(2,1)}, bf16[16,160,1280]{2,1,0:T(8,1...) custom-call(bf16[384,1280]{1,0:T(8,128)(2,1)} %bitcast.11, ...), custom_call_target="tpu_custom_call" | custom-call | tf_op jit(solution)/shard_map/forward/pallas_call | solution.py:903
  130.5 138.6 %backward.1 = (f32[384,1280]{1,0:T(8,128)}, f32[384,1280]{1,0:T(8,128)}, bf16[2,10,80,640]{3,2,1,0:T(8,128)(2,1)}, bf16[2,5,80,384]{3,2,1,0:T(8,128)(2,1)}, f32[2,6,1280]{2,1,0:T(8,128)}) custom-call(s32[1,4]{1,0:T(1,128)} %starts.3, f32[1280]{0:T(1024)} %gain1.3, f32[1280]{0:T(1024)} %gain2.3, bf16[384,1280]{1,0:T(8,128)(2,1)} %bitcast.12, ...), custom_call_target="tpu_custom_call" | custom-call | tf_op jit(solution)/shard_map/backward/pallas_call | solution.py:1527
  269.1 6.5 %finish.1 = (f32[1,384,1280]{2,1,0:T(8,128)}, f32[1,384,1280]{2,1,0:T(8,128)}, f32[80,3840]{1,0:T(8,128)}, f32[80,1280]{1,0:T(8,128)}, f32[80,5120]{1,0:T(8,128)...) custom-call(f32[384,1280]{1,0:T(8,128)} %get-tuple-element.44.raw_ou, ...), custom_call_target="tpu_custom_call" | custom-call | tf_op jit(solution)/shard_map/finish/pallas_call | solution.py:1606
